TPU v7x, 512 devices: a whole 4x8x8 slice. The times are simulated.
512 devices in a mesh: dp: 64 (over y, z), tensor: 8 (over x, core).
Axes of the slice: x: 4, y: 8, z: 8, core: 2. Of those that a mesh axis runs over, the one named last changes fastest.
Arguments:
- normed: bfloat16 [16384, 4608], P(('dp', 'tensor')), may hold values from -32 to 32
- seg_ids: int32 [64, 256], P('dp'), may hold values from 0 to 3, never falling along the last dimension, each value on 1 to 128 neighbouring positions
- w_query: bfloat16 [4608, 2048], P('dp', 'tensor'), may hold values from -0.09375 to 0.09375
- w_key: bfloat16 [4608, 1024], P('dp', 'tensor'), may hold values from -0.09375 to 0.09375
- w_value: bfloat16 [4608, 1024], P('dp', 'tensor'), may hold values from -0.09375 to 0.09375
- grad_attn: bfloat16 [16384, 2048], P('dp', 'tensor'), may hold values from -6 to 6
Outputs:
- input_grad: bfloat16 [16384, 4608], P(('dp', 'tensor'))
- value_weight_grad: float32 [4608, 1024], P('dp', 'tensor')
All inputs are finite; a program needn't handle non-finite values.
Results may differ from a plain program's by a relative error of at most 0.019.
Values may be sent and summed in bfloat16 or wider, within the bound.
A program may use at most 64 MiB of HBM per device.

v0:
```python
import jax
import jax.numpy as jnp
from jax import lax
from jax.sharding import PartitionSpec as P

query_scale = 1.0 / 12.0
masked_value = -1e30


def attention_grads(query, key, value, grad, segments):
    count = query.shape[0]
    head_size = key.shape[1]
    q_heads = query.reshape(count, -1, head_size)
    g_heads = grad.reshape(count, -1, head_size)
    places = jnp.arange(count)
    allowed = (places[None, :] <= places[:, None]) & (segments[:, None] == segments[None, :])
    scores = (
        jnp.einsum("igd,jd->gij", q_heads, key, preferred_element_type=jnp.float32) * query_scale
    )
    scores = jnp.where(allowed[None], scores, masked_value)
    top = jnp.max(scores, axis=-1, keepdims=True)
    expo = jnp.exp(scores - top)
    probs = expo / jnp.sum(expo, axis=-1, keepdims=True)
    probs_b = probs.astype(jnp.bfloat16)
    outputs = jnp.einsum("gij,jd->igd", probs_b, value, preferred_element_type=jnp.float32)
    delta = jnp.sum(g_heads.astype(jnp.float32) * outputs, axis=-1)
    dprobs = jnp.einsum("igd,jd->gij", g_heads, value, preferred_element_type=jnp.float32)
    dscores = (probs * (dprobs - jnp.transpose(delta, (1, 0))[..., None]) * query_scale).astype(
        jnp.bfloat16
    )
    grad_query = jnp.einsum("gij,jd->igd", dscores, key, preferred_element_type=jnp.float32).astype(
        jnp.bfloat16
    )
    grad_key = jnp.einsum(
        "gij,igd->jd", dscores, q_heads, preferred_element_type=jnp.float32
    ).astype(jnp.bfloat16)
    grad_value = jnp.einsum(
        "gij,igd->jd", probs_b, g_heads, preferred_element_type=jnp.float32
    ).astype(jnp.bfloat16)
    return (grad_query.reshape(count, -1), grad_key, grad_value)


def shards(normed, seg_ids, w_query, w_key, w_value, grad_attn):
    gathered = lax.all_gather(normed, "tensor", axis=0, tiled=True)
    full_query, full_key, full_value = (
        lax.all_gather(w_query, "dp", axis=0, tiled=True),
        lax.all_gather(w_key, "dp", axis=0, tiled=True),
        lax.all_gather(w_value, "dp", axis=0, tiled=True),
    )
    query = jnp.dot(gathered, full_query, preferred_element_type=jnp.float32).astype(jnp.bfloat16)
    key = jnp.dot(gathered, full_key, preferred_element_type=jnp.float32).astype(jnp.bfloat16)
    value = jnp.dot(gathered, full_value, preferred_element_type=jnp.float32).astype(jnp.bfloat16)
    segments = seg_ids.reshape(-1)
    grad_query, grad_key, grad_value = attention_grads(query, key, value, grad_attn, segments)
    grad_cat = jnp.concatenate([grad_query, grad_key, grad_value], axis=1)
    weight_cat = jnp.concatenate([full_query, full_key, full_value], axis=1)
    count = gathered.shape[0]
    own_rows = count // lax.axis_size("tensor")
    summed = lax.psum(
        lax.dot_general(
            grad_cat, weight_cat, (((1,), (1,)), ((), ())), preferred_element_type=jnp.float32
        ).astype(jnp.bfloat16),
        "tensor",
    ).astype(jnp.float32)
    input_grad = lax.dynamic_slice_in_dim(
        summed, lax.axis_index("tensor") * own_rows, own_rows, 0
    ).astype(jnp.bfloat16)
    grad_scale = float(count * lax.axis_size("dp")) ** (-0.5)
    value_weight_grad = lax.psum_scatter(
        lax.dot_general(
            gathered, grad_value, (((0,), (0,)), ((), ())), preferred_element_type=jnp.float32
        ),
        "dp",
        scatter_dimension=0,
        tiled=True,
    )
    return (input_grad, value_weight_grad * grad_scale)


def solution(mesh):
    return jax.shard_map(
        shards,
        mesh=mesh,
        in_specs=(
            P(("dp", "tensor"), None),
            P("dp", None),
            P("dp", "tensor"),
            P("dp", "tensor"),
            P("dp", "tensor"),
            P("dp", "tensor"),
        ),
        out_specs=(P(("dp", "tensor"), None), P("dp", "tensor")),
        check_vma=False,
    )
```

profile of v0, /device:TPU:1, one launch (start us, length us, event | category | flops | bytes accessed | tf_op | source)
XLA Modules:
  0.0 553.0 jit_solution(16864351291399390770)
XLA Ops:
  7.2 0.0 all-gather.7.cloned.1.call-start
  7.2 0.7 all-gather.7.cloned.1.call-update
  7.9 0.0 all-gather.5.cloned.1.call-start
  7.9 0.7 all-gather.5.cloned.1.call-update
  8.6 0.0 all-gather.11.cloned.1.call-start
  8.7 0.7 all-gather.11.cloned.1.call-update
  9.4 0.0 all-gather.9.cloned.1.call-start
  9.4 0.5 all-gather.9.cloned.1.call-update
  10.0 0.0 all-reduce.4.cloned.1.call-start
  10.0 1.0 copy.18
  11.0 0.9 fusion.25
  11.9 82.7 %all-gather.7.cloned.1.call-done = bf16[4608,128]{1,0:T(8,128)(2,1)} async-done(((bf16[72,128]{1,0:T(8,128)(2,1)}), bf16[4608,128]{1,0:T(8,128)(2,1)}) %all-gather.7.cloned.1.call-update) | async-done | bytes 1179664 | tf_op jit(solution)/shard_map/all_gather | solution.py:47
  94.6 34.6 %all-gather.5.cloned.1.call-done = bf16[256,4608]{1,0:T(8,128)(2,1)} async-done(((bf16[32,4608]{1,0:T(8,128)(2,1)}), bf16[256,4608]{1,0:T(8,128)(2,1)}) %all-gather.5.cloned.1.call-update) | async-done | bytes 2359312 | tf_op jit(solution)/shard_map/all_gather | solution.py:44
  129.2 0.0 copy-start
  129.2 2.9 fusion.18
  132.1 78.4 %all-gather.11.cloned.1.call-done = bf16[4608,128]{1,0:T(8,128)(2,1)} async-done(((bf16[72,128]{1,0:T(8,128)(2,1)}), bf16[4608,128]{1,0:T(8,128)(2,1)}) %all-gather.11.cloned.1.call-update) | async-done | bytes 1179664 | tf_op jit(solution)/shard_map/all_gather | solution.py:48
  210.4 0.0 copy-done
  210.4 2.0 fusion.19
  212.5 82.8 %all-gather.9.cloned.1.call-done = bf16[4608,256]{1,0:T(8,128)(2,1)} async-done(((bf16[72,256]{1,0:T(8,128)(2,1)}), bf16[4608,256]{1,0:T(8,128)(2,1)}) %all-gather.9.cloned.1.call-update) | async-done | bytes 2359312 | tf_op jit(solution)/shard_map/all_gather | solution.py:46
  295.2 2.7 convolution_convert_fusion.1
  297.9 0.3 fusion.31
  298.2 0.0 copy-start.1
  298.2 0.0 copy-start.2
  298.3 0.0 copy-start.3
  298.3 0.2 fusion.15
  298.5 0.2 fusion.13
  298.8 0.2 convolution_convert_fusion.2
  299.0 0.2 fusion.16
  299.2 0.2 fusion.17
  299.4 0.5 copy-done.1
  299.9 0.3 copy-done.2
  300.2 0.4 copy-done.3
  300.6 2.7 convolution_convert_fusion
  303.3 0.0 all-reduce.4.cloned.1.call-update
  303.3 0.0 all-reduce.6.cloned.1.call-start
  303.4 2.0 convolution_bitcast_fusion
  305.3 0.0 all-reduce.6.cloned.1.call-update
  305.4 1.3 dynamic-slice
  307.3 72.0 %all-reduce.4.cloned.1.call-done = bf16[256,4608]{1,0:T(8,128)(2,1)} async-done(((bf16[256,4608]{1,0:T(8,128)(2,1)}), bf16[256,4608]{1,0:T(8,128)(2,1)}) %all-reduce.4.cloned.1.call-update) | async-done | bytes 2359312 | tf_op jit(solution)/shard_map/psum | solution.py:59
  379.3 1.7 convert_convert_fusion
  381.0 163.5 %all-reduce.6.cloned.1.call-done = f32[4608,128]{0,1:T(8,128)} async-done(((f32[4608,128]{0,1:T(8,128)}), f32[4608,128]{0,1:T(8,128)}) %all-reduce.6.cloned.1.call-update) | async-done | bytes 2359312
  544.5 1.0 dynamic-slice_multiply_fusion
  545.5 0.7 copy.25
  (1 shorter events, 0.0 us)
Async XLA Ops:
  7.2 87.4 %all-gather.7.cloned.1.call-start = ((), (), s32[]{:S(2)}) async-start(), calls=%async_computation.1 | async-start | bytes 1198080 | tf_op jit(solution)/shard_map/all_gather | solution.py:47
  7.9 121.3 %all-gather.5.cloned.1.call-start = ((), (), s32[]{:S(2)}) async-start(), calls=%async_computation | async-start | bytes 2654208 | tf_op jit(solution)/shard_map/all_gather | solution.py:44
  8.6 201.8 %all-gather.11.cloned.1.call-start = ((), (), s32[]{:S(2)}) async-start(), calls=%async_computation.3 | async-start | bytes 1198080 | tf_op jit(solution)/shard_map/all_gather | solution.py:48
  9.4 285.8 %all-gather.9.cloned.1.call-start = ((), (), s32[]{:S(2)}) async-start(), calls=%async_computation.2 | async-start | bytes 2396160 | tf_op jit(solution)/shard_map/all_gather | solution.py:46
  10.0 369.3 %all-reduce.4.cloned.1.call-start = ((), (), s32[]{:S(2)}) async-start(), calls=%async_computation.4 | async-start | bytes 4718592 | tf_op jit(solution)/shard_map/psum | solution.py:59
  129.2 81.3 %copy-start = (bf16[256,4608]{1,0:T(8,128)(2,1)S(1)}, bf16[256,4608]{1,0:T(8,128)(2,1)}, u32[]{:S(2)}) copy-start(bf16[256,4608]{1,0:T(8,128)(2,1)} %all-gather.5.cloned.1.call-done) | copy-start | bytes 7077892
  298.2 1.7 copy-start.1
  298.2 2.0 copy-start.2
  298.3 2.3 copy-start.3
  303.3 241.2 %all-reduce.6.cloned.1.call-start = ((), (), s32[]{:S(2)}) async-start(), calls=%async_computation.5 | async-start | bytes 4718592
Sparse Core Ops, SparseCore 0:
  11.1 83.4 all-gather.6
  96.7 32.4 all-gather.4
  132.2 78.1 all-gather.10
  213.3 81.8 all-gather.8
  303.4 75.8 all-reduce.3
  382.5 162.0 all-reduce.5
where the time goes:
time: 556 us; the launch traced here: 553 us
  waiting for transfers between devices  517 us (93%)
  between operations  14.9 us (3%)
  matrix products  13.7 us (2%)
    unnamed x7, waiting for transfers between devices  166 us
    all_gather x1, waiting for transfers between devices, shards(): lax.all_gather(w_query, 'dp', axis=0, tiled=True)  82.8 us
    all_gather x1, waiting for transfers between devices, shards(): lax.all_gather(w_key, 'dp', axis=0, tiled=True)  82.7 us
    all_gather x1, waiting for transfers between devices, shards(): lax.all_gather(w_value, 'dp', axis=0, tiled=True)  78.4 us
    psum x1, waiting for transfers between devices, shards(): lax.psum(lax.dot_general(grad_cat, weight_cat, (((1,), (1,)), ((), ())),...  72 us
    all_gather x1, waiting for transfers between devices, shards(): gathered = lax.all_gather(normed, 'tensor', axis=0, tiled=True)  34.6 us
  transfers between devices with their start and end apart: 6, of which 6 were waited for; matrix products, arithmetic and copies ran while one was open for 2% of the time, Pallas kernels for 0%

commit v1 on v0

v1 whole, which is shorter than its diff:
```python
import jax
import jax.numpy as jnp
from jax import lax
from jax.experimental import pallas as pl
from jax.experimental.pallas import tpu as pltpu
from jax.sharding import PartitionSpec as P

MESH = pl.DeviceIdType.MESH
F32 = jnp.float32
BF16 = jnp.bfloat16

D = 4608
HD = 128
TOK = 256
RING = 8
XS = 4
ROWS = 72
PAIR = 2 * ROWS
UNIT = RING * ROWS
HALF = D // 2
CHUNK = 2 * UNIT
CHUNKS = D // CHUNK
OWN = 32
LOW, HIGH, HIGH_PAD = 32, 40, 48
QUERY_SCALE = 1.0 / 12.0
MASKED = -1e30
RIGHT, LEFT = 0, 1
SIGN = (1, -1)

NT = (((1,), (1,)), ((), ()))


def dot(a, b):
    return jnp.dot(a, b, preferred_element_type=F32)


def dot_nt(a, b):
    return lax.dot_general(a, b, NT, preferred_element_type=F32)


def kernel(
    normed, seg, w_query, w_key, w_value, grad,
    input_grad, value_grad,
    x_buf, x_t, w_buf, pair_out, pair_in, mask, q_acc, kv_acc, g_cat,
    vw, a_send, a_recv, b_send, b_recv, a_sum, b_sum, a_low, b_high, a_got, b_got,
    part, sib, far_send, far_recv, near_send, near_recv,
    pair_s, pair_r, x_s, x_r, a1_s, a1_r, b1_s, b1_r, a2f_s, b2f_s, a2_s, b2_s, a2_r, b2_r,
    va_s, va_r, vb_s, vb_r, vd_s, vd_r, sib_s, sib_r, far_s, far_r, near_s, near_r,
):
    dp, tensor = lax.axis_index("dp"), lax.axis_index("tensor")
    y, z, x, core = dp // RING, dp % RING, tensor // 2, tensor % 2
    par, m = z % 2, z // 2
    other = 1 - core

    def at(xx, yy, zz, cc):
        return (yy * RING + zz, xx * 2 + cc)

    def shift(position, by, size=RING):
        return (position + by + size) % size

    def y_dev(by):
        return at(x, shift(y, by), z, core)

    def z_dev(by):
        return at(x, y, shift(z, by), core)

    def x_dev(by):
        return at(shift(x, by, XS), y, z, core)

    sibling = at(x, y, z, other)
    partner = at(x, y, z + 1 - 2 * par, core)
    sent = []

    def copy(src, dst, send_sem, recv_sem, device):
        return pltpu.make_async_remote_copy(
            src_ref=src, dst_ref=dst, send_sem=send_sem, recv_sem=recv_sem, device_id=device, device_id_type=MESH
        )

    def send(src, dst, send_sem, recv_sem, device):
        one = copy(src, dst, send_sem, recv_sem, device)
        one.start()
        sent.append(one)

    def arrived(dst, send_sem, recv_sem):
        copy(dst, dst, send_sem, recv_sem, sibling).wait_recv()

    def drain(count):
        for _ in range(count):
            sent.pop(0).wait_send()

    barrier = pltpu.get_barrier_semaphore()
    friends = [sibling, x_dev(1), x_dev(-1)]
    friends += [y_dev(by) for by in range(1, RING)] + [z_dev(by) for by in range(1, RING)]
    for friend in friends:
        pl.semaphore_signal(barrier, inc=1, device_id=friend, device_id_type=MESH)

    q_first, q_second = w_query[:, :HD].astype(F32), w_query[:, HD:].astype(F32)
    k_own, v_own = w_key[...].astype(F32), w_value[...].astype(F32)
    even = par == 0
    keep_q, give_q = jnp.where(even, q_first, q_second), jnp.where(even, q_second, q_first)
    keep_kv, give_kv = jnp.where(even, k_own, v_own), jnp.where(even, v_own, k_own)
    pair_out[...] = jnp.concatenate([give_q, give_kv], axis=0).astype(BF16)

    pl.semaphore_wait(barrier, len(friends))
    send(pair_out, pair_in, pair_s, pair_r, partner)

    def rows_of(xx, cc):
        return pl.ds(pl.multiple_of((2 * xx + cc) * OWN, OWN), OWN)

    here = x_buf.at[rows_of(x, core)]
    send(normed, here, x_s.at[0], x_r.at[0], x_dev(1))
    send(normed, here, x_s.at[1], x_r.at[1], x_dev(-1))
    send(normed, here, x_s.at[2], x_r.at[2], sibling)
    x_buf[rows_of(x, core), :] = normed[...]

    seg_f = seg[...].astype(F32)
    seg_col = jnp.transpose(jnp.broadcast_to(seg_f, (HD, TOK)))
    seg_col = jnp.concatenate([seg_col, seg_col], axis=1)
    key_at = lax.broadcasted_iota(jnp.int32, (TOK, TOK), 0)
    query_at = lax.broadcasted_iota(jnp.int32, (TOK, TOK), 1)
    mask[...] = jnp.where((key_at <= query_at) & (seg_col == seg_f), 1.0, 0.0).astype(F32)

    def unit_a(zz):
        return w_buf.at[zz % 2, y, pl.ds(pl.multiple_of((zz // 2) * PAIR, 16), PAIR)]

    def unit_b(yy):
        return w_buf.at[2 + par, yy, pl.ds(pl.multiple_of(m * PAIR, 16), PAIR)]

    def piece_a(yy, k):
        return w_buf.at[k, yy]

    def piece_b(zz, k):
        return w_buf.at[2 + zz % 2, pl.ds(4 * k, 4), pl.ds(pl.multiple_of((zz // 2) * PAIR, 16), PAIR)]

    arrived(pair_in, pair_s, pair_r)
    got = pair_in[...].astype(F32)
    got_q, got_kv = got[:ROWS], got[ROWS:]
    own_rows = pl.ds(pl.multiple_of(m * PAIR, 16), PAIR)
    w_buf[par, y, own_rows, :] = jnp.where(
        even, jnp.concatenate([keep_q, got_q], axis=0), jnp.concatenate([got_q, keep_q], axis=0)
    ).astype(BF16)
    w_buf[2 + par, y, own_rows, :] = jnp.where(
        even, jnp.concatenate([keep_kv, got_kv], axis=0), jnp.concatenate([got_kv, keep_kv], axis=0)
    ).astype(BF16)

    def first_hop(way, hop):
        by = SIGN[way]
        zz, yy = shift(z, -by * (hop - 1)), shift(y, -by * (hop - 1))
        send(unit_a(zz), unit_a(zz), a1_s.at[way, hop - 1], a1_r.at[way, hop - 1], z_dev(by))
        send(unit_b(yy), unit_b(yy), b1_s.at[way, hop - 1], b1_r.at[way, hop - 1], y_dev(by))

    def turn(zz, yy, index):
        for way in (RIGHT, LEFT):
            by = SIGN[way]
            send(unit_a(zz), unit_a(zz), a2f_s.at[way, index], a2_r.at[way, 0, zz % 2], y_dev(by))
            send(unit_b(yy), unit_b(yy), b2f_s.at[way, index], b2_r.at[way, 0, yy // 4], z_dev(by))

    first_hop(RIGHT, 1)
    first_hop(LEFT, 1)
    turn(z, y, 0)
    index = 0
    for hop in range(1, 5):
        for way in (RIGHT, LEFT):
            if way == LEFT and hop == 4:
                continue
            by = SIGN[way]
            zz, yy = shift(z, -by * hop), shift(y, -by * hop)
            arrived(unit_a(zz), a1_s.at[way, hop - 1], a1_r.at[way, hop - 1])
            arrived(unit_b(yy), b1_s.at[way, hop - 1], b1_r.at[way, hop - 1])
            if hop + 1 <= (4 if way == RIGHT else 3):
                first_hop(way, hop + 1)
            index += 1
            turn(zz, yy, index)

    left_half, right_half = pl.ds(0, HALF), pl.ds(HALF, HALF)
    x_right, x_left, x_far = shift(x, 1, XS), shift(x, -1, XS), shift(x, 2, XS)

    def x_ref(xx, cc, columns=None):
        return x_buf.at[rows_of(xx, cc)] if columns is None else x_buf.at[rows_of(xx, cc), columns]

    def x_forward():
        arrived(x_ref(x_left, core), x_s.at[0], x_r.at[0])
        send(x_ref(x_left, core, left_half), x_ref(x_left, core, left_half), x_s.at[3], x_r.at[3], x_dev(1))
        send(x_ref(x_left, core), x_ref(x_left, core), x_s.at[4], x_r.at[4], sibling)
        arrived(x_ref(x_right, core), x_s.at[1], x_r.at[1])
        send(x_ref(x_right, core, right_half), x_ref(x_right, core, right_half), x_s.at[5], x_r.at[5], x_dev(-1))
        send(x_ref(x_right, core), x_ref(x_right, core), x_s.at[6], x_r.at[6], sibling)

    def x_finish():
        arrived(x_ref(x_far, core, left_half), x_s.at[3], x_r.at[3])
        send(x_ref(x_far, core, left_half), x_ref(x_far, core, left_half), x_s.at[7], x_r.at[7], sibling)
        arrived(x_ref(x_far, core, right_half), x_s.at[5], x_r.at[5])
        send(x_ref(x_far, core, right_half), x_ref(x_far, core, right_half), x_s.at[8], x_r.at[8], sibling)
        arrived(x_ref(x, other), x_s.at[2], x_r.at[2])
        arrived(x_ref(x_left, other), x_s.at[4], x_r.at[4])
        arrived(x_ref(x_right, other), x_s.at[6], x_r.at[6])
        arrived(x_ref(x_far, other, left_half), x_s.at[7], x_r.at[7])
        arrived(x_ref(x_far, other, right_half), x_s.at[8], x_r.at[8])

    def pass_on(hop):
        for k in range(2):
            for way in (RIGHT, LEFT):
                by = SIGN[way]
                yy, zz = shift(y, -by * hop), shift(z, -by * hop)
                if hop == 4 and k != way:
                    continue
                arrived(piece_a(yy, k), a2_s.at[way, 0, k], a2_r.at[way, hop - 1, k])
                if hop < 3 or (hop == 3 and k == way):
                    send(piece_a(yy, k), piece_a(yy, k), a2_s.at[way, hop - 1, k], a2_r.at[way, hop, k], y_dev(by))
                arrived(piece_b(zz, k), b2_s.at[way, 0, k], b2_r.at[way, hop - 1, k])
                if hop < 3 or (hop == 3 and k == way):
                    send(piece_b(zz, k), piece_b(zz, k), b2_s.at[way, hop - 1, k], b2_r.at[way, hop, k], z_dev(by))

    def x_columns(p):
        return x_buf[:, pl.ds(pl.multiple_of(p * CHUNK, HD), CHUNK)]

    def weights(kinds, p):
        return jnp.concatenate([w_buf[kind, pl.ds(2 * p, 2)].reshape(CHUNK, HD) for kind in kinds], axis=1)

    p_own = y // 2
    p_step = 1 - 2 * ((y + 1) % 2)

    x_forward()
    older = len(sent)
    pass_on(1)
    x_finish()
    drain(older)
    older = len(sent)
    q_acc[...] = dot(x_columns(p_own), weights((0, 1), p_own))

    pass_on(2)
    p_next = shift(p_own, p_step, CHUNKS)
    q_acc[...] += dot(x_columns(p_next), weights((0, 1), p_next))

    def flip(i, carry):
        columns = pl.ds(pl.multiple_of(i * 4 * HD, 4 * HD), 4 * HD)
        x_t[columns, :] = jnp.transpose(x_buf[:, columns])
        return carry

    lax.fori_loop(0, D // (4 * HD), flip, 0)
    drain(older)
    older = len(sent)

    pass_on(3)
    p_next = shift(p_own, -p_step, CHUNKS)
    q_acc[...] += dot(x_columns(p_next), weights((0, 1), p_next))
    drain(older)
    pass_on(4)
    p_next = shift(p_own, 2, CHUNKS)
    query = (q_acc[...] + dot(x_columns(p_next), weights((0, 1), p_next))).astype(BF16)

    kv_acc[...] = jnp.zeros_like(kv_acc)

    def project(p, carry):
        kv_acc[...] += dot(x_columns(p), weights((2, 3), p))
        return carry

    lax.fori_loop(0, CHUNKS, project, 0)
    key, value = kv_acc[:, :HD].astype(BF16), kv_acc[:, HD:].astype(BF16)

    allowed = mask[...] > 0.5
    probs, dprobs = [], []
    for h in range(2):
        scores = jnp.where(allowed, dot_nt(key, query[:, h * HD : (h + 1) * HD]) * QUERY_SCALE, MASKED)
        expo = jnp.exp(scores - jnp.max(scores, axis=0, keepdims=True))
        probs.append(expo * (1.0 / jnp.sum(expo, axis=0, keepdims=True)))
        dprobs.append(dot_nt(value, grad[:, h * HD : (h + 1) * HD]))
    rounded = [one.astype(BF16) for one in probs]
    grad_v = (dot(rounded[0], grad[:, :HD]) + dot(rounded[1], grad[:, HD:])).astype(BF16)

    for yy in range(RING):
        vw[yy] = dot(x_t[yy * UNIT : (yy + 1) * UNIT, :], grad_v).reshape(RING, ROWS, HD)

    def vw_low(yy, k):
        return vw[yy, 4 * k : 4 * k + 4, :LOW, :]

    def vw_high(zz, k):
        return vw[4 * k : 4 * k + 4, zz, LOW:, :]

    def pad(block):
        return jnp.concatenate([block, jnp.zeros((4, HIGH_PAD - HIGH, HD), F32)], axis=1)

    def vw_step(step, k, way):
        by = SIGN[way]
        low, high = vw_low(shift(y, by * (5 - step)), k), vw_high(shift(z, by * (5 - step)), k)
        if step > 2 or (step == 2 and k == way):
            arrived(a_recv.at[way, step - 2, k], va_s.at[way, step - 2, k], va_r.at[way, step - 2, k])
            arrived(b_recv.at[way, step - 2, k], vb_s.at[way, step - 2, k], vb_r.at[way, step - 2, k])
            low = low + a_recv[way, step - 2, k].astype(F32)
            high = high + b_recv[way, step - 2, k][:, :HIGH, :].astype(F32)
        a_send[way, step - 1, k] = low.astype(BF16)
        b_send[way, step - 1, k] = pad(high).astype(BF16)
        slot = (way, step - 1, k)
        send(a_send.at[slot], a_recv.at[slot], va_s.at[slot], va_r.at[slot], y_dev(by))
        send(b_send.at[slot], b_recv.at[slot], vb_s.at[slot], vb_r.at[slot], z_dev(by))

    def vw_turn():
        for k in range(2):
            low, high = vw_low(y, k), vw_high(z, k)
            for way in (RIGHT, LEFT):
                slot = (way, 3, k)
                arrived(a_recv.at[slot], va_s.at[slot], va_r.at[slot])
                arrived(b_recv.at[slot], vb_s.at[slot], vb_r.at[slot])
                low = low + a_recv[slot].astype(F32)
                high = high + b_recv[slot][:, :HIGH, :].astype(F32)
            a_sum[4 * k : 4 * k + 4] = low
            b_sum[4 * k : 4 * k + 4] = high
            a_low[4 * k : 4 * k + 4] = low.astype(BF16)
            b_high[4 * k : 4 * k + 4] = pad(high).astype(BF16)
        for by in range(1, RING):
            zz, yy = shift(z, by), shift(y, by)
            send(a_low.at[zz], a_got.at[by - 1], vd_s.at[0, by - 1], vd_r.at[0, by - 1], z_dev(by))
            send(b_high.at[yy], b_got.at[by - 1], vd_s.at[1, by - 1], vd_r.at[1, by - 1], y_dev(by))

    def vw_finish():
        low, high = a_sum[z], b_sum[y]
        for by in range(1, RING):
            arrived(a_got.at[by - 1], vd_s.at[0, by - 1], vd_r.at[0, by - 1])
            arrived(b_got.at[by - 1], vd_s.at[1, by - 1], vd_r.at[1, by - 1])
            low = low + a_got[by - 1].astype(F32)
            high = high + b_got[by - 1][:HIGH].astype(F32)
        scale = float(TOK * RING * RING) ** (-0.5)
        value_grad[:LOW, :] = low * scale
        value_grad[LOW:, :] = high * scale

    for way in (RIGHT, LEFT):
        vw_step(1, way, way)
    for way in (RIGHT, LEFT):
        vw_step(2, 1 - way, way)

    dscores = []
    for h in range(2):
        delta = jnp.sum(rounded[h].astype(F32) * dprobs[h], axis=0, keepdims=True)
        dscores.append((probs[h] * (dprobs[h] - delta) * QUERY_SCALE).astype(BF16))
    key_t = jnp.transpose(key)
    for h in range(2):
        g_cat[:, h * HD : (h + 1) * HD] = jnp.transpose(dot(key_t, dscores[h])).astype(BF16)
    g_cat[:, 2 * HD : 3 * HD] = (dot(dscores[0], query[:, :HD]) + dot(dscores[1], query[:, HD:])).astype(BF16)
    g_cat[:, 3 * HD :] = grad_v

    def ig_part(q):
        both = dot_nt(g_cat[...], weights((0, 1, 2, 3), q)).astype(BF16)
        part[q] = both.reshape(XS, 2, OWN, CHUNK)
        send(part.at[q, :, other], sib.at[q], sib_s.at[q], sib_r.at[q], sibling)

    def chip_sum(q, xx):
        return part[q, xx, core].astype(F32) + sib[q, xx].astype(F32)

    def ig_first(q):
        way = q % 2
        by = SIGN[way]
        arrived(sib.at[q], sib_s.at[q], sib_r.at[q])
        far_send[q] = chip_sum(q, x_far).astype(BF16)
        send(far_send.at[q], far_recv.at[q], far_s.at[q], far_r.at[q], x_dev(by))
        near_send[q, 1 - way] = chip_sum(q, shift(x, -by, XS)).astype(BF16)
        slot = (q, 1 - way)
        send(near_send.at[slot], near_recv.at[slot], near_s.at[slot], near_r.at[slot], x_dev(-by))

    def ig_second(q):
        way = q % 2
        by = SIGN[way]
        arrived(far_recv.at[q], far_s.at[q], far_r.at[q])
        near_send[q, way] = (chip_sum(q, shift(x, by, XS)) + far_recv[q].astype(F32)).astype(BF16)
        slot = (q, way)
        send(near_send.at[slot], near_recv.at[slot], near_s.at[slot], near_r.at[slot], x_dev(by))

    def ig_finish(q):
        total = chip_sum(q, x)
        for way in (RIGHT, LEFT):
            slot = (q, way)
            arrived(near_recv.at[slot], near_s.at[slot], near_r.at[slot])
            total = total + near_recv[slot].astype(F32)
        input_grad[:, q * CHUNK : (q + 1) * CHUNK] = total.astype(BF16)

    ig_part(0)
    ig_part(1)
    ig_first(0)
    for way in (RIGHT, LEFT):
        vw_step(2, way, way)
    ig_part(2)
    ig_first(1)
    ig_part(3)
    ig_first(2)
    ig_first(3)
    for k in range(2):
        for way in (RIGHT, LEFT):
            vw_step(3, k, way)
    ig_second(0)
    ig_second(1)
    for k in range(2):
        for way in (RIGHT, LEFT):
            vw_step(4, k, way)
    ig_second(2)
    ig_second(3)
    older = len(sent)
    vw_turn()
    drain(older)
    ig_finish(0)
    ig_finish(1)
    vw_finish()
    ig_finish(2)
    ig_finish(3)
    drain(len(sent))


def shards(normed, seg_ids, w_query, w_key, w_value, grad_attn):
    vmem = pl.BlockSpec(memory_space=pltpu.VMEM)
    dma = pltpu.SemaphoreType.DMA
    scratch = [
        pltpu.VMEM((TOK, D), BF16),
        pltpu.VMEM((D, TOK), BF16),
        pltpu.VMEM((4, RING, UNIT, HD), BF16),
        pltpu.VMEM((PAIR, HD), BF16),
        pltpu.VMEM((PAIR, HD), BF16),
        pltpu.VMEM((TOK, TOK), F32),
        pltpu.VMEM((TOK, 2 * HD), F32),
        pltpu.VMEM((TOK, 2 * HD), F32),
        pltpu.VMEM((TOK, 4 * HD), BF16),
        pltpu.VMEM((RING, RING, ROWS, HD), F32),
        pltpu.VMEM((2, 4, 2, 4, LOW, HD), BF16),
        pltpu.VMEM((2, 4, 2, 4, LOW, HD), BF16),
        pltpu.VMEM((2, 4, 2, 4, HIGH_PAD, HD), BF16),
        pltpu.VMEM((2, 4, 2, 4, HIGH_PAD, HD), BF16),
        pltpu.VMEM((RING, LOW, HD), F32),
        pltpu.VMEM((RING, HIGH, HD), F32),
        pltpu.VMEM((RING, LOW, HD), BF16),
        pltpu.VMEM((RING, HIGH_PAD, HD), BF16),
        pltpu.VMEM((RING - 1, LOW, HD), BF16),
        pltpu.VMEM((RING - 1, HIGH_PAD, HD), BF16),
        pltpu.VMEM((CHUNKS, XS, 2, OWN, CHUNK), BF16),
        pltpu.VMEM((CHUNKS, XS, OWN, CHUNK), BF16),
        pltpu.VMEM((CHUNKS, OWN, CHUNK), BF16),
        pltpu.VMEM((CHUNKS, OWN, CHUNK), BF16),
        pltpu.VMEM((CHUNKS, 2, OWN, CHUNK), BF16),
        pltpu.VMEM((CHUNKS, 2, OWN, CHUNK), BF16),
        dma(()), dma(()),
        dma((9,)), dma((9,)),
        dma((2, 4)), dma((2, 4)),
        dma((2, 4)), dma((2, 4)),
        dma((2, RING)), dma((2, RING)),
        dma((2, 3, 2)), dma((2, 3, 2)),
        dma((2, 4, 2)), dma((2, 4, 2)),
        dma((2, 4, 2)), dma((2, 4, 2)),
        dma((2, 4, 2)), dma((2, 4, 2)),
        dma((2, RING - 1)), dma((2, RING - 1)),
        dma((CHUNKS,)), dma((CHUNKS,)),
        dma((CHUNKS,)), dma((CHUNKS,)),
        dma((CHUNKS, 2)), dma((CHUNKS, 2)),
    ]
    return pl.pallas_call(
        kernel,
        out_shape=(jax.ShapeDtypeStruct((OWN, D), BF16), jax.ShapeDtypeStruct((ROWS, HD), F32)),
        in_specs=[vmem] * 6,
        out_specs=(vmem, vmem),
        scratch_shapes=scratch,
        compiler_params=pltpu.CompilerParams(
            collective_id=0, has_side_effects=True, vmem_limit_bytes=50 * 1024 * 1024
        ),
        name="attention_backward",
    )(normed, seg_ids, w_query, w_key, w_value, grad_attn)


def solution(mesh):
    return jax.shard_map(
        shards,
        mesh=mesh,
        in_specs=(
            P(("dp", "tensor"), None),
            P("dp", None),
            P("dp", "tensor"),
            P("dp", "tensor"),
            P("dp", "tensor"),
            P("dp", "tensor"),
        ),
        out_specs=(P(("dp", "tensor"), None), P("dp", "tensor")),
        check_vma=False,
    )
```

time: 556 us -> 85.1 us (0.15)
  waiting for transfers between devices: 517 us -> 0 us
  Pallas kernels: 0 us -> 77.1 us
  between operations: 14.9 us -> 0.65 us
  matrix products: 13.7 us -> 0 us
    all_gather x4 -> x0, waiting for transfers between devices: 278 us -> none  [the longest x1 82.8 us: shards(): lax.all_gather(w_query, 'dp', axis=0, tiled=True)]
    unnamed x7 -> x0, waiting for transfers between devices: 166 us -> none
    pallas_call x0 -> x1, Pallas kernels: none -> 77.1 us  [shards(): pl.pallas_call(kernel, out_shape=(jax.ShapeDtypeStruct((OWN, D), BF16), j...]
    psum x1 -> x0, waiting for transfers between devices: 72 us -> none  [shards(): lax.psum(lax.dot_general(grad_cat, weight_cat, (((1,), (1,)), ((), ())),...]
    dot_general x10 -> x0, matrix products: 13.4 us -> none  [the longest x1 2.89 us: shards(): jnp.dot(gathered, full_key, preferred_element_type=jnp.float32)]
  transfers between devices with their start and end apart: 6 -> 0, of which waited for: 6 -> 0; matrix products, arithmetic and copies ran while one was open for 2% -> 0% of each run, Pallas kernels for 0% -> 0%
where the time goes in v1:
time: 85.1 us; the launch traced here: 83.9 us
  Pallas kernels  77.1 us (91%)
  local copies, waits for them, and re-layouts  6.08 us (7%)
    pallas_call x1, Pallas kernels, shards(): pl.pallas_call(kernel, out_shape=(jax.ShapeDtypeStruct((OWN, D), BF16), j...  77.1 us
    unnamed x14, local copies, waits for them, and re-layouts  6.08 us

profile of v1, /device:TPU:1, one launch (start us, length us, event | category | flops | bytes accessed | tf_op | source)
XLA Modules:
  0.0 83.9 jit_solution(13212084528320738719)
XLA Ops:
  0.6 0.0 copy-start
  0.6 1.0 %copy-done = bf16[32,4608]{1,0:T(8,128)(2,1)S(1)} copy-done((bf16[32,4608]{1,0:T(8,128)(2,1)S(1)}, bf16[32,4608]{1,0:T(8,128)(2,1)}, u32[]{:S(2)}) %copy-start) | copy-done | bytes 294936
  1.6 0.0 copy-start.1
  1.6 0.9 %copy-done.1 = bf16[256,256]{1,0:T(8,128)(2,1)S(1)} copy-done((bf16[256,256]{1,0:T(8,128)(2,1)S(1)}, bf16[256,256]{1,0:T(8,128)(2,1)}, u32[]{:S(2)}) %copy-start.1) | copy-done | bytes 131096
  2.5 0.0 copy-start.2
  2.5 0.8 copy-done.2
  3.3 0.0 copy-start.3
  3.3 0.7 copy-done.3
  4.0 0.0 copy-start.4
  4.0 0.7 copy-done.4
  4.7 0.0 copy-start.5
  4.7 0.7 copy-done.5
  5.4 77.1 %attention_backward.1 = (bf16[32,4608]{1,0:T(8,128)(2,1)S(1)}, f32[72,128]{1,0:T(8,128)S(1)}) custom-call(bf16[32,4608]{1,0:T(8,128)(2,1)S(1)} %copy-done, s32[1,256]{1,0:T(1,128)S(1)} %copy-done.5, bf16[72,256]{1,0:T(8,128)(2,1)S(1)} %copy-done.2, bf16[72,128]{1,0:T(8,128)(2,1)S(1)} %copy-done.3, bf16[72,128]{1,0:T(8,128)(2,1)S(1)} %copy-done.4, ...), custom_call_target="tpu_custom_call" | custom-call | tf_op jit(solution)/shard_map/attention_backward/pallas_call | solution.py:450
  82.5 0.7 copy.10
  83.3 0.6 copy.11
Async XLA Ops:
  0.6 1.0 %copy-start = (bf16[32,4608]{1,0:T(8,128)(2,1)S(1)}, bf16[32,4608]{1,0:T(8,128)(2,1)}, u32[]{:S(2)}) copy-start(bf16[32,4608]{1,0:T(8,128)(2,1)} %normed.1) | copy-start | bytes 884740
  1.6 0.9 %copy-start.1 = (bf16[256,256]{1,0:T(8,128)(2,1)S(1)}, bf16[256,256]{1,0:T(8,128)(2,1)}, u32[]{:S(2)}) copy-start(bf16[256,256]{1,0:T(8,128)(2,1)} %grad.1) | copy-start | bytes 393220
  2.5 0.8 copy-start.2
  3.3 0.7 copy-start.3
  4.0 0.7 copy-start.4
  4.7 0.7 copy-start.5

commit v2 on v1

v2 whole, which is shorter than its diff:
```python
import jax
import jax.numpy as jnp
from jax import lax
from jax.experimental import pallas as pl
from jax.experimental.pallas import tpu as pltpu
from jax.sharding import PartitionSpec as P

MESH = pl.DeviceIdType.MESH
F32 = jnp.float32
BF16 = jnp.bfloat16

D = 4608
HD = 128
TOK = 256
RING = 8
XS = 4
ROWS = 72
PAIR = 2 * ROWS
UNIT = RING * ROWS
HALF = D // 2
CHUNK = 2 * UNIT
CHUNKS = D // CHUNK
OWN = 32
PADDED = 80
ENTRIES = (0, -1, 1, -2, 2, -3, 3, -4)
GROUP = 4
QUERY_SCALE = 1.0 / 12.0
MASKED = -1e30
RIGHT, LEFT = 0, 1
SIGN = (1, -1)

NT = (((1,), (1,)), ((), ()))


def dot(a, b):
    return jnp.dot(a, b, preferred_element_type=F32)


def dot_nt(a, b):
    return lax.dot_general(a, b, NT, preferred_element_type=F32)


def kernel(
    normed, seg_hbm, w_query_hbm, w_key_hbm, w_value_hbm, grad_hbm,
    input_grad, value_grad,
    seg, w_query, w_key, w_value, grad,
    x_buf, x_t, x_p, w_buf, pair_out, pair_in, mask, q_acc, kv_acc, g_cat,
    vw, a_send, a_recv, b_send, b_recv, line_sum, line_send, line_recv,
    part, sib, far_send, far_recv, near_send, near_recv,
    in_sem, pair_s, pair_r, x_s, x_r, turn_s, turn_r, pass_s, a_r, b_r,
    v_s, va_r, vb_r, line_s, line_r, sib_s, sib_r, far_s, far_r, near_s, near_r,
):
    dp, tensor = lax.axis_index("dp"), lax.axis_index("tensor")
    y, z, x, core = dp // RING, dp % RING, tensor // 2, tensor % 2
    par, m = z % 2, z // 2
    other = 1 - core

    def at(xx, yy, zz, cc):
        return (yy * RING + zz, xx * 2 + cc)

    def shift(position, by, size=RING):
        return (position + by + size) % size

    def y_dev(by):
        return at(x, shift(y, by), z, core)

    def z_dev(by):
        return at(x, y, shift(z, by), core)

    def x_dev(by):
        return at(shift(x, by, XS), y, z, core)

    sibling = at(x, y, z, other)
    partner = at(x, y, z + 1 - 2 * par, core)

    def copy(src, dst, send_sem, recv_sem, device):
        return pltpu.make_async_remote_copy(
            src_ref=src, dst_ref=dst, send_sem=send_sem, recv_sem=recv_sem, device_id=device, device_id_type=MESH
        )

    def send(src, dst, send_sem, recv_sem, device):
        copy(src, dst, send_sem, recv_sem, device).start()

    def arrived(like, recv_sem):
        copy(like, like, pair_s, recv_sem, sibling).wait_recv()

    def left(like, send_sem):
        copy(like, like, send_sem, pair_r, sibling).wait_send()

    barrier = pltpu.get_barrier_semaphore()
    friends = [sibling, x_dev(1), x_dev(-1)]
    friends += [y_dev(by) for by in range(1, RING)] + [z_dev(by) for by in range(1, RING)]
    for friend in friends:
        pl.semaphore_signal(barrier, inc=1, device_id=friend, device_id_type=MESH)

    def rows_of(xx, cc):
        return pl.ds(pl.multiple_of((2 * xx + cc) * OWN, OWN), OWN)

    here = x_buf.at[rows_of(x, core)]
    local = [
        pltpu.make_async_copy(src, dst, in_sem.at[i])
        for i, (src, dst) in enumerate(
            [(w_query_hbm, w_query), (w_key_hbm, w_key), (w_value_hbm, w_value), (normed, here), (seg_hbm, seg), (grad_hbm, grad)]
        )
    ]
    for one in local:
        one.start()

    for one in local[:3]:
        one.wait()
    q_first, q_second = w_query[:, :HD].astype(F32), w_query[:, HD:].astype(F32)
    k_own, v_own = w_key[...].astype(F32), w_value[...].astype(F32)
    even = par == 0
    keep_q, give_q = jnp.where(even, q_first, q_second), jnp.where(even, q_second, q_first)
    keep_kv, give_kv = jnp.where(even, k_own, v_own), jnp.where(even, v_own, k_own)
    pair_out[...] = jnp.concatenate([give_q, give_kv], axis=0).astype(BF16)

    pl.semaphore_wait(barrier, len(friends))
    send(pair_out, pair_in, pair_s, pair_r, partner)
    for one in local[3:]:
        one.wait()
    send(here, here, x_s, x_r.at[0], x_dev(1))
    send(here, here, x_s, x_r.at[1], x_dev(-1))
    send(here, here, x_s, x_r.at[4], sibling)

    seg_f = seg[...].astype(F32)
    seg_col = jnp.transpose(jnp.broadcast_to(seg_f, (HD, TOK)))
    seg_col = jnp.concatenate([seg_col, seg_col], axis=1)
    key_at = lax.broadcasted_iota(jnp.int32, (TOK, TOK), 0)
    query_at = lax.broadcasted_iota(jnp.int32, (TOK, TOK), 1)
    mask[...] = jnp.where((key_at <= query_at) & (seg_col == seg_f), 1.0, 0.0).astype(F32)

    def pair_rows(pair):
        return pl.ds(pl.multiple_of(pair * PAIR, 16), PAIR)

    def unit_a(yy, zz):
        return w_buf.at[zz % 2, yy, pair_rows(zz // 2)]

    def unit_b(yy, zz):
        return w_buf.at[2 + zz % 2, yy, pair_rows(zz // 2)]

    arrived(pair_in, pair_r)
    got = pair_in[...].astype(F32)
    got_q, got_kv = got[:ROWS], got[ROWS:]
    w_buf[par, y, pair_rows(m), :] = jnp.where(
        even, jnp.concatenate([keep_q, got_q], axis=0), jnp.concatenate([got_q, keep_q], axis=0)
    ).astype(BF16)
    w_buf[2 + par, y, pair_rows(m), :] = jnp.where(
        even, jnp.concatenate([keep_kv, got_kv], axis=0), jnp.concatenate([got_kv, keep_kv], axis=0)
    ).astype(BF16)

    def first_hop(way, hop):
        by = SIGN[way]
        zz, yy = shift(z, -by * (hop - 1)), shift(y, -by * (hop - 1))
        slot = (way, hop - 1)
        send(unit_a(y, zz), unit_a(y, zz), turn_s, turn_r.at[(0,) + slot], z_dev(by))
        send(unit_b(yy, z), unit_b(yy, z), turn_s, turn_r.at[(1,) + slot], y_dev(by))

    def turn(entry):
        zz, yy = shift(z, ENTRIES[entry]), shift(y, ENTRIES[entry])
        for way in (RIGHT, LEFT):
            by, slot = SIGN[way], (way, 0, entry // GROUP)
            send(unit_a(y, zz), unit_a(y, zz), pass_s, a_r.at[slot], y_dev(by))
            send(unit_b(yy, z), unit_b(yy, z), pass_s, b_r.at[slot], z_dev(by))

    def first_arrived(hop):
        ways = (RIGHT, LEFT) if hop < 4 else (RIGHT,)
        for way in ways:
            for kind in range(2):
                arrived(pair_in, turn_r.at[kind, way, hop - 1])
            if hop + 1 <= (4 if way == RIGHT else 3):
                first_hop(way, hop + 1)
        for way in ways:
            turn(2 * hop - 1 + way)

    group_bytes = w_buf.at[0, 0]

    def pass_on(hop, group):
        for way in (RIGHT, LEFT):
            by = SIGN[way]
            yy, zz = shift(y, -by * hop), shift(z, -by * hop)
            entries = [GROUP * group + i for i in range(GROUP) if hop < 3 or i % 2 == way]
            slot = (way, hop, group) if hop < 3 else (RIGHT, 3, group)
            arrived(group_bytes, a_r.at[way, hop - 1, group])
            for entry in entries:
                unit = unit_a(yy, shift(z, ENTRIES[entry]))
                send(unit, unit, pass_s, a_r.at[slot], y_dev(by))
            arrived(group_bytes, b_r.at[way, hop - 1, group])
            for entry in entries:
                unit = unit_b(shift(y, ENTRIES[entry]), zz)
                send(unit, unit, pass_s, b_r.at[slot], z_dev(by))

    def pass_end(group):
        arrived(group_bytes, a_r.at[RIGHT, 3, group])
        arrived(group_bytes, b_r.at[RIGHT, 3, group])

    left_half, right_half = pl.ds(0, HALF), pl.ds(HALF, HALF)
    x_right, x_left, x_far = shift(x, 1, XS), shift(x, -1, XS), shift(x, 2, XS)

    def x_block(xx, columns=None):
        rows = rows_of(xx, core)
        return x_buf.at[rows] if columns is None else x_buf.at[rows, columns]

    def x_forward():
        arrived(here, x_r.at[0])
        send(x_block(x_left, left_half), x_block(x_left, left_half), x_s, x_r.at[2], x_dev(1))
        arrived(here, x_r.at[1])
        send(x_block(x_right, right_half), x_block(x_right, right_half), x_s, x_r.at[3], x_dev(-1))
        send(x_block(x_left), x_block(x_left), x_s, x_r.at[4], sibling)
        send(x_block(x_right), x_block(x_right), x_s, x_r.at[4], sibling)

    def x_finish():
        for way, columns in ((2, left_half), (3, right_half)):
            arrived(x_block(x_far, columns), x_r.at[way])
            send(x_block(x_far, columns), x_block(x_far, columns), x_s, x_r.at[4], sibling)
        arrived(x_buf.at[pl.ds(0, XS * OWN)], x_r.at[4])

    def flip(i, carry):
        columns = pl.ds(pl.multiple_of(i * CHUNK, HD), CHUNK)
        x_t[pl.ds(2 * i, 2)] = jnp.transpose(x_buf[:, columns]).reshape(2, 4, PAIR, TOK)
        return carry

    def flip_back(i, carry):
        x_p[i] = jnp.transpose(x_t[:, i].reshape(CHUNK, TOK))
        return carry

    def weights(kinds, p):
        return jnp.concatenate([w_buf[kind, pl.ds(2 * p, 2)].reshape(CHUNK, HD) for kind in kinds], axis=1)

    def q_product(p):
        return dot(x_buf[:, pl.ds(pl.multiple_of(p * CHUNK, HD), CHUNK)], weights((0, 1), p))

    def kv_product(p):
        both = [w_buf[kind, :, pair_rows(p), :].reshape(CHUNK, HD) for kind in (2, 3)]
        return dot(x_p[p], jnp.concatenate(both, axis=1))

    def order(position):
        near = 1 - 2 * ((position + 1) % 2)
        pair = position // 2
        return [pair, shift(pair, near, CHUNKS), shift(pair, -near, CHUNKS), shift(pair, 2, CHUNKS)]

    y_pairs, z_pairs = order(y), order(z)

    first_hop(RIGHT, 1)
    first_hop(LEFT, 1)
    turn(0)
    first_arrived(1)
    first_arrived(2)
    first_arrived(3)
    x_forward()
    pass_on(1, 0)
    first_arrived(4)
    pass_on(1, 1)
    pass_on(2, 0)
    x_finish()
    q_acc[...] = q_product(y_pairs[0])
    lax.fori_loop(0, CHUNKS, flip, 0)
    pass_on(2, 1)
    lax.fori_loop(0, CHUNKS, flip_back, 0)
    kv_acc[...] = kv_product(z_pairs[0])
    q_acc[...] += q_product(y_pairs[1])
    kv_acc[...] += kv_product(z_pairs[1])
    left(pair_out, pair_s)
    left(x_buf.at[pl.ds(0, 7 * OWN)], x_s)
    left(w_buf.at[0, pl.ds(0, 7), pl.ds(0, 2 * PAIR)], turn_s)
    pass_on(3, 0)
    pass_on(3, 1)
    q_acc[...] += q_product(y_pairs[2])
    kv_acc[...] += kv_product(z_pairs[2])
    pass_end(0)
    pass_end(1)
    kv = kv_acc[...] + kv_product(z_pairs[3])
    key, value = kv[:, :HD].astype(BF16), kv[:, HD:].astype(BF16)
    query = (q_acc[...] + q_product(y_pairs[3])).astype(BF16)

    allowed = mask[...] > 0.5
    probs, dprobs = [], []
    for h in range(2):
        scores = jnp.where(allowed, dot_nt(key, query[:, h * HD : (h + 1) * HD]) * QUERY_SCALE, MASKED)
        expo = jnp.exp(scores - jnp.max(scores, axis=0, keepdims=True))
        probs.append(expo * (1.0 / jnp.sum(expo, axis=0, keepdims=True)))
        dprobs.append(dot_nt(value, grad[:, h * HD : (h + 1) * HD]))
    rounded = [one.astype(BF16) for one in probs]
    grad_v = (dot(rounded[0], grad[:, :HD]) + dot(rounded[1], grad[:, HD:])).astype(BF16)

    for yy in range(RING):
        vw[yy // 2, yy % 2] = dot(x_t[yy].reshape(UNIT, TOK), grad_v).reshape(RING, ROWS, HD)

    def vw_y(yy, k):
        return vw[yy // 2, yy % 2, pl.ds(4 * (yy % 2) + 2 * k, 2)].reshape(PAIR, HD)

    def vw_z(zz, k):
        return vw[2 * k : 2 * k + 2, 1 - zz // 4, zz].reshape(PAIR, HD)

    def vw_step(step, long):
        for way in (RIGHT, LEFT):
            by, k = SIGN[way], way if long else 1 - way
            for own, position, sends, recvs, sems, device in (
                (vw_y, y, a_send, a_recv, va_r, y_dev(by)),
                (vw_z, z, b_send, b_recv, vb_r, z_dev(by)),
            ):
                total = own(shift(position, by * (5 - step)), k)
                if step > 2 or (step == 2 and long):
                    arrived(pair_in, sems.at[step - 2, k, way])
                    total = total + recvs[step - 2, k, way].astype(F32)
                slot = (step - 1, k, way)
                sends[slot] = total.astype(BF16)
                send(sends.at[slot], recvs.at[slot], v_s, sems.at[slot], device)

    y_first = z // 4 == y % 2

    def vw_turn():
        for base, own, position, recvs, sems in ((0, vw_y, y, a_recv, va_r), (4, vw_z, z, b_recv, vb_r)):
            for k in range(2):
                total = own(position, k)
                for way in (RIGHT, LEFT):
                    arrived(pair_in, sems.at[3, k, way])
                    total = total + recvs[3, k, way].astype(F32)
                total = total.reshape(2, ROWS, HD)
                line_sum[base + 2 * k : base + 2 * k + 2] = total
                padded = jnp.concatenate([total, jnp.zeros((2, PADDED - ROWS, HD), F32)], axis=1)
                line_send[base + 2 * k : base + 2 * k + 2] = padded.astype(BF16)
        for_line(True)

    def for_line(start):
        for i in range(4):
            zz, yy = 4 * (y % 2) + i, 2 * i + 1 - z // 4
            one = copy(line_send.at[i], line_recv.at[z], line_s.at[i], line_r, at(x, y, zz, core))
            two = copy(line_send.at[4 + i], line_recv.at[y], line_s.at[4 + i], line_r, at(x, yy, z, core))
            pl.when(zz != z)(one.start if start else one.wait_send)
            pl.when(yy != y)(two.start if start else two.wait_send)

    def vw_finish():
        arrived(line_recv.at[pl.ds(0, RING - 1)], line_r)
        position = jnp.where(y_first, z, y)
        total = line_sum[jnp.where(y_first, z % 4, 4 + y // 2)]
        for by in range(1, RING):
            total = total + line_recv[shift(position, by)].astype(F32)[:ROWS]
        value_grad[...] = total * float(TOK * RING * RING) ** (-0.5)

    vw_step(1, True)
    vw_step(2, False)

    dscores = []
    for h in range(2):
        delta = jnp.sum(rounded[h].astype(F32) * dprobs[h], axis=0, keepdims=True)
        dscores.append((probs[h] * (dprobs[h] - delta) * QUERY_SCALE).astype(BF16))
    key_t = jnp.transpose(key)
    for h in range(2):
        g_cat[:, h * HD : (h + 1) * HD] = jnp.transpose(dot(key_t, dscores[h])).astype(BF16)
    g_cat[:, 2 * HD : 3 * HD] = (dot(dscores[0], query[:, :HD]) + dot(dscores[1], query[:, HD:])).astype(BF16)
    g_cat[:, 3 * HD :] = grad_v

    def ig_part(q):
        both = dot_nt(g_cat[...], weights((0, 1, 2, 3), q)).astype(BF16)
        part[q] = both.reshape(XS, 2, OWN, CHUNK)
        send(part.at[q, :, other], sib.at[q], sib_s, sib_r.at[q], sibling)

    def chip_sum(q, xx):
        return part[q, xx, core].astype(F32) + sib[q, xx].astype(F32)

    def near(q, way):
        send(near_send.at[q, way], near_recv.at[q, way], near_s, near_r.at[q], x_dev(SIGN[way]))

    def ig_first(q):
        way = q % 2
        by = SIGN[way]
        arrived(sib.at[q], sib_r.at[q])
        far_send[q] = chip_sum(q, x_far).astype(BF16)
        send(far_send.at[q], far_recv.at[q], far_s, far_r.at[q], x_dev(by))
        near_send[q, 1 - way] = chip_sum(q, shift(x, -by, XS)).astype(BF16)
        near(q, 1 - way)

    def ig_second(q):
        way = q % 2
        arrived(far_recv.at[q], far_r.at[q])
        near_send[q, way] = (chip_sum(q, shift(x, SIGN[way], XS)) + far_recv[q].astype(F32)).astype(BF16)
        near(q, way)

    def ig_finish(q):
        total = chip_sum(q, x)
        arrived(near_recv.at[q], near_r.at[q])
        for way in (RIGHT, LEFT):
            total = total + near_recv[q, way].astype(F32)
        input_grad[:, q * CHUNK : (q + 1) * CHUNK] = total.astype(BF16)

    ig_part(0)
    ig_part(1)
    vw_step(2, True)
    ig_first(0)
    vw_step(3, False)
    ig_part(2)
    ig_first(1)
    ig_part(3)
    ig_first(2)
    vw_step(3, True)
    ig_first(3)
    vw_step(4, False)
    ig_second(0)
    ig_second(1)
    vw_step(4, True)
    ig_second(2)
    ig_second(3)
    vw_turn()
    left(w_buf.at[:, pl.ds(0, 7)], pass_s)
    left(w_buf.at[0, pl.ds(0, 7)], v_s)
    left(sib, sib_s)
    left(far_send, far_s)
    ig_finish(0)
    ig_finish(1)
    ig_finish(2)
    ig_finish(3)
    vw_finish()
    left(near_send, near_s)
    for_line(False)


def shards(*args):
    vmem = pl.BlockSpec(memory_space=pltpu.VMEM)
    dma = pltpu.SemaphoreType.DMA
    scratch = [
        pltpu.VMEM((1, TOK), jnp.int32),
        pltpu.VMEM((ROWS, 2 * HD), BF16),
        pltpu.VMEM((ROWS, HD), BF16),
        pltpu.VMEM((ROWS, HD), BF16),
        pltpu.VMEM((TOK, 2 * HD), BF16),
        pltpu.VMEM((TOK, D), BF16),
        pltpu.VMEM((RING, 4, PAIR, TOK), BF16),
        pltpu.VMEM((CHUNKS, TOK, CHUNK), BF16),
        pltpu.VMEM((4, RING, UNIT, HD), BF16),
        pltpu.VMEM((PAIR, HD), BF16),
        pltpu.VMEM((PAIR, HD), BF16),
        pltpu.VMEM((TOK, TOK), F32),
        pltpu.VMEM((TOK, 2 * HD), F32),
        pltpu.VMEM((TOK, 2 * HD), F32),
        pltpu.VMEM((TOK, 4 * HD), BF16),
        pltpu.VMEM((RING // 2, 2, RING, ROWS, HD), F32),
        pltpu.VMEM((4, 2, 2, PAIR, HD), BF16),
        pltpu.VMEM((4, 2, 2, PAIR, HD), BF16),
        pltpu.VMEM((4, 2, 2, PAIR, HD), BF16),
        pltpu.VMEM((4, 2, 2, PAIR, HD), BF16),
        pltpu.VMEM((RING, ROWS, HD), F32),
        pltpu.VMEM((RING, PADDED, HD), BF16),
        pltpu.VMEM((RING, PADDED, HD), BF16),
        pltpu.VMEM((CHUNKS, XS, 2, OWN, CHUNK), BF16),
        pltpu.VMEM((CHUNKS, XS, OWN, CHUNK), BF16),
        pltpu.VMEM((CHUNKS, OWN, CHUNK), BF16),
        pltpu.VMEM((CHUNKS, OWN, CHUNK), BF16),
        pltpu.VMEM((CHUNKS, 2, OWN, CHUNK), BF16),
        pltpu.VMEM((CHUNKS, 2, OWN, CHUNK), BF16),
        dma((6,)),
        dma(()), dma(()),
        dma(()), dma((5,)),
        dma(()), dma((2, 2, 4)),
        dma(()), dma((2, 4, 2)), dma((2, 4, 2)),
        dma(()), dma((4, 2, 2)), dma((4, 2, 2)),
        dma((RING,)), dma(()),
        dma(()), dma((CHUNKS,)),
        dma(()), dma((CHUNKS,)),
        dma(()), dma((CHUNKS,)),
    ]
    hbm = pl.BlockSpec(memory_space=pltpu.HBM)
    return pl.pallas_call(
        kernel,
        out_shape=(jax.ShapeDtypeStruct((OWN, D), BF16), jax.ShapeDtypeStruct((ROWS, HD), F32)),
        in_specs=[hbm] * 6,
        out_specs=(vmem, vmem),
        scratch_shapes=scratch,
        compiler_params=pltpu.CompilerParams(
            collective_id=0, has_side_effects=True, vmem_limit_bytes=50 * 1024 * 1024
        ),
        name="attention_backward",
    )(*[pltpu.with_memory_space_constraint(one, pltpu.HBM) for one in args])


def solution(mesh):
    return jax.shard_map(
        shards,
        mesh=mesh,
        in_specs=(
            P(("dp", "tensor"), None),
            P("dp", None),
            P("dp", "tensor"),
            P("dp", "tensor"),
            P("dp", "tensor"),
            P("dp", "tensor"),
        ),
        out_specs=(P(("dp", "tensor"), None), P("dp", "tensor")),
        check_vma=False,
    )
```

time: 85.1 us -> 73.5 us (0.86)
  Pallas kernels: 77.1 us -> 70.1 us
  local copies, waits for them, and re-layouts: 6.08 us -> 1.33 us
    pallas_call x1, Pallas kernels: 77.1 us -> 70.1 us  [shards(): pl.pallas_call(kernel, out_shape=(jax.ShapeDtypeStruct((OWN, D), BF16), j...]
    unnamed x14 -> x2, local copies, waits for them, and re-layouts: 6.08 us -> 1.33 us
where the time goes in v2:
time: 73.5 us; the launch traced here: 72 us
  Pallas kernels  70.1 us (95%)
  local copies, waits for them, and re-layouts  1.33 us (2%)
    pallas_call x1, Pallas kernels, shards(): pl.pallas_call(kernel, out_shape=(jax.ShapeDtypeStruct((OWN, D), BF16), j...  70.1 us

profile of v2, /device:TPU:1, one launch (start us, length us, event | category | flops | bytes accessed | tf_op | source)
XLA Modules:
  0.0 72.0 jit_solution(13642662752965786991)
XLA Ops:
  0.6 70.1 %attention_backward.1 = (bf16[32,4608]{1,0:T(8,128)(2,1)S(1)}, f32[72,128]{1,0:T(8,128)S(1)}) custom-call(bf16[32,4608]{1,0:T(8,128)(2,1)} %normed.1, s32[1,256]{1,0:T(1,128)} %seg_hbm.1, bf16[72,256]{1,0:T(8,128)(2,1)} %w_query_hbm.1, bf16[72,128]{1,0:T(8,128)(2,1)} %w_key_hbm.1, bf16[72,128]{1,0:T(8,128)(2,1)} %w_value_hbm.1, bf16[256,256]{1,0:T(8,128)(2,1)} %grad_hbm.1), custom_call_target="tpu_custom_call" | custom-call | tf_op jit(solution)/shard_map/attention_backward/pallas_call | solution.py:463
  70.7 0.7 copy.10
  71.4 0.6 copy.11

commit v3 on v2

v3 whole, which is shorter than its diff:
```python
import jax
import jax.numpy as jnp
from jax import lax
from jax.experimental import pallas as pl
from jax.experimental.pallas import tpu as pltpu
from jax.sharding import PartitionSpec as P

MESH = pl.DeviceIdType.MESH
F32 = jnp.float32
BF16 = jnp.bfloat16

D = 4608
HD = 128
TOK = 256
RING = 8
XS = 4
ROWS = 72
PAIR = 2 * ROWS
UNIT = RING * ROWS
HALF = D // 2
CHUNK = 2 * UNIT
CHUNKS = D // CHUNK
OWN = 32
PADDED = 80
ENTRIES = (0, -1, 1, -2, 2, -3, 3, -4)
GROUP = 2
QUERY_SCALE = 1.0 / 12.0
MASKED = -1e30
RIGHT, LEFT = 0, 1
SIGN = (1, -1)

NT = (((1,), (1,)), ((), ()))


def dot(a, b):
    return jnp.dot(a, b, preferred_element_type=F32)


def dot_nt(a, b):
    return lax.dot_general(a, b, NT, preferred_element_type=F32)


def kernel(
    normed, seg_hbm, w_query, w_key, w_value, grad_hbm,
    input_grad, value_grad,
    seg, grad, x_buf, x_t, x_p, w_raw, w_buf, mask, q_acc, kv_acc, g_cat,
    vw, v_send, v_recv, line_sum, line_send, line_recv,
    part, sib, far_send, far_recv, near_send, near_recv,
    in_sem, x_s, x_r, first_s, first_r, pass_s, a_r, b_r, a_end, b_end,
    v_s, v_r, line_s, line_r, sib_s, sib_r, far_s, far_r, near_s, near_r,
):
    dp, tensor = lax.axis_index("dp"), lax.axis_index("tensor")
    y, z, x, core = dp // RING, dp % RING, tensor // 2, tensor % 2
    other = 1 - core

    def at(xx, yy, zz, cc):
        return (yy * RING + zz, xx * 2 + cc)

    def shift(position, by, size=RING):
        return (position + by + size) % size

    def y_dev(by):
        return at(x, shift(y, by), z, core)

    def z_dev(by):
        return at(x, y, shift(z, by), core)

    def x_dev(by):
        return at(shift(x, by, XS), y, z, core)

    sibling = at(x, y, z, other)

    def copy(src, dst, send_sem, recv_sem, device):
        return pltpu.make_async_remote_copy(
            src_ref=src, dst_ref=dst, send_sem=send_sem, recv_sem=recv_sem, device_id=device, device_id_type=MESH
        )

    def send(src, dst, send_sem, recv_sem, device):
        copy(src, dst, send_sem, recv_sem, device).start()

    def arrived(like, recv_sem):
        copy(like, like, first_s, recv_sem, sibling).wait_recv()

    def left(like, send_sem):
        copy(like, like, send_sem, line_r, sibling).wait_send()

    barrier = pltpu.get_barrier_semaphore()
    friends = [sibling, x_dev(1), x_dev(-1)]
    friends += [y_dev(by) for by in range(1, RING)] + [z_dev(by) for by in range(1, RING)]
    for friend in friends:
        pl.semaphore_signal(barrier, inc=1, device_id=friend, device_id_type=MESH)

    def rows_of(xx, cc):
        return pl.ds(pl.multiple_of((2 * xx + cc) * OWN, OWN), OWN)

    here = x_buf.at[rows_of(x, core)]
    own = [w_query.at[:, :HD], w_query.at[:, HD:], w_key, w_value]
    own_a, own_b = w_raw.at[0, y, z], w_raw.at[1, y, z]
    local = [
        pltpu.make_async_copy(src, dst, in_sem.at[i])
        for src, dst, i in (
            (own[0], own_a.at[0], 0), (own[1], own_a.at[1], 0), (own[2], own_b.at[0], 1), (own[3], own_b.at[1], 1),
            (normed, here, 2), (seg_hbm, seg, 3), (grad_hbm, grad, 4),
        )
    ]
    for one in local:
        one.start()

    pl.semaphore_wait(barrier, len(friends))

    def send_own(route, entry, device):
        for i in range(2):
            send(own[2 * route + i], w_raw.at[route, y, z, i], first_s, first_r.at[route, entry], device)

    def turn_own():
        for i in range(2):
            for way in (RIGHT, LEFT):
                by = SIGN[way]
                send(own[i], own_a.at[i], pass_s, a_r.at[way, 0, 0], y_dev(by))
                send(own[2 + i], own_b.at[i], pass_s, b_r.at[way, 0, 0], z_dev(by))

    for entry in (1, 2):
        send_own(0, entry, z_dev(-ENTRIES[entry]))
        send_own(1, entry, y_dev(-ENTRIES[entry]))
    turn_own()
    for entry in range(3, 7):
        send_own(0, entry, z_dev(-ENTRIES[entry]))
        send_own(1, entry, y_dev(-ENTRIES[entry]))

    send(normed, here, x_s, x_r.at[0], x_dev(1))
    send(normed, here, x_s, x_r.at[1], x_dev(-1))
    send(normed, here, x_s, x_r.at[4], sibling)
    pltpu.make_async_copy(own_a, own_a, in_sem.at[0]).wait()
    pltpu.make_async_copy(own_b, own_b, in_sem.at[1]).wait()
    for one in local[4:]:
        one.wait()

    seg_f = seg[...].astype(F32)
    seg_col = jnp.transpose(jnp.broadcast_to(seg_f, (HD, TOK)))
    seg_col = jnp.concatenate([seg_col, seg_col], axis=1)
    key_at = lax.broadcasted_iota(jnp.int32, (TOK, TOK), 0)
    query_at = lax.broadcasted_iota(jnp.int32, (TOK, TOK), 1)
    mask[...] = jnp.where((key_at <= query_at) & (seg_col == seg_f), 1.0, 0.0).astype(F32)

    def unit_a(yy, zz):
        return w_raw.at[0, yy, zz]

    def unit_b(yy, zz):
        return w_raw.at[1, yy, zz]

    def turn(entry):
        zz, yy = shift(z, ENTRIES[entry]), shift(y, ENTRIES[entry])
        for way in (RIGHT, LEFT):
            by, slot = SIGN[way], (way, 0, entry // GROUP)
            send(unit_a(y, zz), unit_a(y, zz), pass_s, a_r.at[slot], y_dev(by))
            send(unit_b(yy, z), unit_b(yy, z), pass_s, b_r.at[slot], z_dev(by))

    def relay(way):
        by = SIGN[way]
        zz, yy = shift(z, -2 * by), shift(y, -2 * by)
        one, two = unit_a(y, zz).at[way], unit_b(yy, z).at[way]
        send(one, one, first_s, first_r.at[0, 7], z_dev(2 * by))
        send(two, two, first_s, first_r.at[1, 7], y_dev(2 * by))

    def first_arrived(entry):
        for route in range(2):
            arrived(own_a, first_r.at[route, entry])
        if entry in (3, 4):
            relay(entry - 3)
        turn(entry)

    group_bytes = w_raw.at[0, 0, pl.ds(0, GROUP)]

    def pass_on(hop, group):
        for way in (RIGHT, LEFT):
            by = SIGN[way]
            yy, zz = shift(y, -by * hop), shift(z, -by * hop)
            entries = [GROUP * group + i for i in range(GROUP) if hop < 3 or i % 2 == way]
            arrived(group_bytes, a_r.at[way, hop - 1, group])
            for entry in entries:
                unit = unit_a(yy, shift(z, ENTRIES[entry]))
                send(unit, unit, pass_s, a_r.at[way, hop, group] if hop < 3 else a_end.at[group], y_dev(by))
            arrived(group_bytes, b_r.at[way, hop - 1, group])
            for entry in entries:
                unit = unit_b(shift(y, ENTRIES[entry]), zz)
                send(unit, unit, pass_s, b_r.at[way, hop, group] if hop < 3 else b_end.at[group], z_dev(by))

    def pass_end(group):
        arrived(group_bytes, a_end.at[group])
        arrived(group_bytes, b_end.at[group])

    left_half, right_half = pl.ds(0, HALF), pl.ds(HALF, HALF)
    x_right, x_left, x_far = shift(x, 1, XS), shift(x, -1, XS), shift(x, 2, XS)

    def x_block(xx, columns=None):
        rows = rows_of(xx, core)
        return x_buf.at[rows] if columns is None else x_buf.at[rows, columns]

    def x_forward():
        arrived(here, x_r.at[0])
        send(x_block(x_left, left_half), x_block(x_left, left_half), x_s, x_r.at[2], x_dev(1))
        arrived(here, x_r.at[1])
        send(x_block(x_right, right_half), x_block(x_right, right_half), x_s, x_r.at[3], x_dev(-1))
        send(x_block(x_left), x_block(x_left), x_s, x_r.at[4], sibling)
        send(x_block(x_right), x_block(x_right), x_s, x_r.at[4], sibling)

    def x_finish():
        for way, columns in ((2, left_half), (3, right_half)):
            arrived(x_block(x_far, columns), x_r.at[way])
            send(x_block(x_far, columns), x_block(x_far, columns), x_s, x_r.at[4], sibling)
        arrived(x_buf.at[pl.ds(0, XS * OWN)], x_r.at[4])

    def flip(i, carry):
        columns = pl.ds(pl.multiple_of(i * CHUNK, HD), CHUNK)
        x_t[pl.ds(2 * i, 2)] = jnp.transpose(x_buf[:, columns]).reshape(2, 4, PAIR, TOK)
        return carry

    def flip_back(i, carry):
        x_p[i] = jnp.transpose(x_t[:, i].reshape(CHUNK, TOK))
        return carry

    def weights(kinds, p):
        return jnp.concatenate([w_buf[kind, pl.ds(2 * p, 2)].reshape(CHUNK, HD) for kind in kinds], axis=1)

    def q_product(p):
        both = []
        for i in range(2):
            block = w_raw[0, pl.ds(2 * p, 2), :, i].astype(F32).reshape(CHUNK, HD).astype(BF16)
            w_buf[i, pl.ds(2 * p, 2)] = block.reshape(2, UNIT, HD)
            both.append(block)
        return dot(x_buf[:, pl.ds(pl.multiple_of(p * CHUNK, HD), CHUNK)], jnp.concatenate(both, axis=1))

    def kv_product(p):
        both = []
        for i in range(2):
            block = w_raw[1, :, pl.ds(2 * p, 2), i].astype(F32).reshape(CHUNK, HD).astype(BF16)
            w_buf[2 + i, :, pl.ds(pl.multiple_of(p * PAIR, 16), PAIR), :] = block.reshape(RING, PAIR, HD)
            both.append(block)
        return dot(x_p[p], jnp.concatenate(both, axis=1))

    def order(position):
        near = 1 - 2 * ((position + 1) % 2)
        pair = position // 2
        return [pair, shift(pair, near, CHUNKS), shift(pair, -near, CHUNKS), shift(pair, 2, CHUNKS)]

    y_pairs, z_pairs = order(y), order(z)

    for entry in range(1, 7):
        first_arrived(entry)
    pass_on(1, 0)
    first_arrived(7)
    pass_on(1, 1)
    x_forward()
    pass_on(1, 2)
    pass_on(2, 0)
    pass_on(1, 3)
    pass_on(2, 1)
    pass_on(2, 2)
    pass_on(3, 0)
    pass_on(2, 3)
    x_finish()
    q_acc[...] = q_product(y_pairs[0])
    pass_on(3, 1)
    lax.fori_loop(0, CHUNKS, flip, 0)
    pass_on(3, 2)
    lax.fori_loop(0, CHUNKS, flip_back, 0)
    pass_on(3, 3)
    left(w_raw.at[:, 0, pl.ds(0, 7)], first_s)
    left(x_buf.at[pl.ds(0, 7 * OWN)], x_s)
    kv_acc[...] = kv_product(z_pairs[0])
    q_acc[...] += q_product(y_pairs[1])
    kv_acc[...] += kv_product(z_pairs[1])
    q_acc[...] += q_product(y_pairs[2])
    kv_acc[...] += kv_product(z_pairs[2])
    for group in range(RING // GROUP):
        pass_end(group)
    kv = kv_acc[...] + kv_product(z_pairs[3])
    key, value = kv[:, :HD].astype(BF16), kv[:, HD:].astype(BF16)
    query = (q_acc[...] + q_product(y_pairs[3])).astype(BF16)

    allowed = mask[...] > 0.5
    probs, dprobs = [], []
    for h in range(2):
        scores = jnp.where(allowed, dot_nt(key, query[:, h * HD : (h + 1) * HD]) * QUERY_SCALE, MASKED)
        expo = jnp.exp(scores - jnp.max(scores, axis=0, keepdims=True))
        probs.append(expo * (1.0 / jnp.sum(expo, axis=0, keepdims=True)))
        dprobs.append(dot_nt(value, grad[:, h * HD : (h + 1) * HD]))
    rounded = [one.astype(BF16) for one in probs]
    grad_v = (dot(rounded[0], grad[:, :HD]) + dot(rounded[1], grad[:, HD:])).astype(BF16)

    for yy in range(RING):
        vw[yy // 2, yy % 2] = dot(x_t[yy].reshape(UNIT, TOK), grad_v).reshape(RING, ROWS, HD)

    def vw_y(yy, k):
        return vw[yy // 2, yy % 2, pl.ds(4 * (yy % 2) + 2 * k, 2)].reshape(PAIR, HD)

    def vw_z(zz, k):
        return vw[2 * k : 2 * k + 2, 1 - zz // 4, zz].reshape(PAIR, HD)

    routes = ((vw_y, y, y_dev), (vw_z, z, z_dev))

    def vw_send(route, way, slot, device):
        v_s_r = v_r.at[route, way, slot]
        send(v_send.at[route, way, slot], v_recv.at[route, way, slot], v_s, v_s_r, device)

    def vw_first():
        for way in (RIGHT, LEFT):
            by = SIGN[way]
            for route, (own_part, position, device) in enumerate(routes):
                v_send[route, way, 0] = own_part(shift(position, 4 * by), way).astype(BF16)
                vw_send(route, way, 0, device(2 * by))
                for slot, k in ((1, 1 - way), (2, way)):
                    v_send[route, way, slot] = own_part(shift(position, 3 * by), k).astype(BF16)
                    vw_send(route, way, slot, device(by))

    def vw_near():
        for way in (RIGHT, LEFT):
            by = SIGN[way]
            for route, (own_part, position, device) in enumerate(routes):
                for k in range(2):
                    v_send[route, way, 5 + k] = own_part(shift(position, by), k).astype(BF16)
                    vw_send(route, way, 5 + k, device(by))

    def vw_second():
        for way in (RIGHT, LEFT):
            by = SIGN[way]
            for route, (own_part, position, device) in enumerate(routes):
                for slot, k, gets in ((3, 1 - way, (1,)), (4, way, (0, 2))):
                    total = own_part(shift(position, 2 * by), k)
                    for got in gets:
                        arrived(v_send.at[0, 0, 0], v_r.at[route, way, got])
                        total = total + v_recv[route, way, got].astype(F32)
                    v_send[route, way, slot] = total.astype(BF16)
                    vw_send(route, way, slot, device(2 * by))

    y_first = z // 4 == y % 2

    def vw_turn():
        for route, (own_part, position, _) in enumerate(routes):
            for k in range(2):
                total = own_part(position, k)
                for way in (RIGHT, LEFT):
                    for slot in (5 + k, 4 if k == way else 3):
                        arrived(v_send.at[0, 0, 0], v_r.at[route, way, slot])
                        total = total + v_recv[route, way, slot].astype(F32)
                total = total.reshape(2, ROWS, HD)
                at_rows = pl.ds(4 * route + 2 * k, 2)
                line_sum[at_rows] = total
                padded = jnp.concatenate([total, jnp.zeros((2, PADDED - ROWS, HD), F32)], axis=1)
                line_send[at_rows] = padded.astype(BF16)
        for i in range(4):
            zz, yy = 4 * (y % 2) + i, 2 * i + 1 - z // 4
            one = copy(line_send.at[i], line_recv.at[z], line_s, line_r, at(x, y, zz, core))
            two = copy(line_send.at[4 + i], line_recv.at[y], line_s, line_r, at(x, yy, z, core))
            pl.when(zz != z)(one.start)
            pl.when(yy != y)(two.start)

    def vw_finish():
        arrived(line_recv.at[pl.ds(0, RING - 1)], line_r)
        position = jnp.where(y_first, z, y)
        total = line_sum[jnp.where(y_first, z % 4, 4 + y // 2)]
        for by in range(1, RING):
            total = total + line_recv[shift(position, by)].astype(F32)[:ROWS]
        value_grad[...] = total * float(TOK * RING * RING) ** (-0.5)

    vw_first()
    vw_near()

    dscores = []
    for h in range(2):
        delta = jnp.sum(rounded[h].astype(F32) * dprobs[h], axis=0, keepdims=True)
        dscores.append((probs[h] * (dprobs[h] - delta) * QUERY_SCALE).astype(BF16))
    key_t = jnp.transpose(key)
    for h in range(2):
        g_cat[:, h * HD : (h + 1) * HD] = jnp.transpose(dot(key_t, dscores[h])).astype(BF16)
    g_cat[:, 2 * HD : 3 * HD] = (dot(dscores[0], query[:, :HD]) + dot(dscores[1], query[:, HD:])).astype(BF16)
    g_cat[:, 3 * HD :] = grad_v

    def ig_part(q):
        both = dot_nt(g_cat[...], weights((0, 1, 2, 3), q)).astype(BF16)
        part[q] = both.reshape(XS, 2, OWN, CHUNK)
        send(part.at[q, :, other], sib.at[q], sib_s, sib_r.at[q], sibling)

    def chip_sum(q, xx):
        return part[q, xx, core].astype(F32) + sib[q, xx].astype(F32)

    def near(q, way):
        send(near_send.at[q, way], near_recv.at[q, way], near_s, near_r.at[q], x_dev(SIGN[way]))

    def ig_far(q):
        arrived(sib.at[q], sib_r.at[q])
        far_send[q] = chip_sum(q, x_far).astype(BF16)
        send(far_send.at[q], far_recv.at[q], far_s, far_r.at[q], x_dev(SIGN[q % 2]))

    def ig_near(q):
        way = 1 - q % 2
        near_send[q, way] = chip_sum(q, shift(x, SIGN[way], XS)).astype(BF16)
        near(q, way)

    def ig_second(q):
        way = q % 2
        arrived(far_recv.at[q], far_r.at[q])
        near_send[q, way] = (chip_sum(q, shift(x, SIGN[way], XS)) + far_recv[q].astype(F32)).astype(BF16)
        near(q, way)

    def ig_finish(q):
        total = chip_sum(q, x)
        arrived(near_recv.at[q], near_r.at[q])
        for way in (RIGHT, LEFT):
            total = total + near_recv[q, way].astype(F32)
        input_grad[:, q * CHUNK : (q + 1) * CHUNK] = total.astype(BF16)

    ig_part(0)
    ig_part(1)
    ig_part(2)
    ig_far(0)
    ig_part(3)
    ig_far(1)
    ig_far(2)
    ig_near(0)
    ig_near(1)
    ig_far(3)
    ig_near(2)
    ig_near(3)
    vw_second()
    ig_second(0)
    ig_second(1)
    ig_second(2)
    ig_second(3)
    vw_turn()
    left(w_raw.at[:, :, pl.ds(0, 7)], pass_s)
    left(v_send, v_s)
    left(sib, sib_s)
    left(far_send, far_s)
    ig_finish(0)
    ig_finish(1)
    vw_finish()
    left(line_recv.at[pl.ds(0, RING - 1)], line_s)
    ig_finish(2)
    ig_finish(3)
    left(near_send, near_s)


def shards(*args):
    vmem = pl.BlockSpec(memory_space=pltpu.VMEM)
    dma = pltpu.SemaphoreType.DMA
    scratch = [
        pltpu.VMEM((1, TOK), jnp.int32),
        pltpu.VMEM((TOK, 2 * HD), BF16),
        pltpu.VMEM((TOK, D), BF16),
        pltpu.VMEM((RING, 4, PAIR, TOK), BF16),
        pltpu.VMEM((CHUNKS, TOK, CHUNK), BF16),
        pltpu.VMEM((2, RING, RING, 2, ROWS, HD), BF16),
        pltpu.VMEM((4, RING, UNIT, HD), BF16),
        pltpu.VMEM((TOK, TOK), F32),
        pltpu.VMEM((TOK, 2 * HD), F32),
        pltpu.VMEM((TOK, 2 * HD), F32),
        pltpu.VMEM((TOK, 4 * HD), BF16),
        pltpu.VMEM((RING // 2, 2, RING, ROWS, HD), F32),
        pltpu.VMEM((2, 2, 7, PAIR, HD), BF16),
        pltpu.VMEM((2, 2, 7, PAIR, HD), BF16),
        pltpu.VMEM((RING, ROWS, HD), F32),
        pltpu.VMEM((RING, PADDED, HD), BF16),
        pltpu.VMEM((RING, PADDED, HD), BF16),
        pltpu.VMEM((CHUNKS, XS, 2, OWN, CHUNK), BF16),
        pltpu.VMEM((CHUNKS, XS, OWN, CHUNK), BF16),
        pltpu.VMEM((CHUNKS, OWN, CHUNK), BF16),
        pltpu.VMEM((CHUNKS, OWN, CHUNK), BF16),
        pltpu.VMEM((CHUNKS, 2, OWN, CHUNK), BF16),
        pltpu.VMEM((CHUNKS, 2, OWN, CHUNK), BF16),
        dma((5,)),
        dma(()), dma((5,)),
        dma(()), dma((2, RING)),
        dma(()), dma((2, 3, 4)), dma((2, 3, 4)), dma((4,)), dma((4,)),
        dma(()), dma((2, 2, 7)),
        dma(()), dma(()),
        dma(()), dma((CHUNKS,)),
        dma(()), dma((CHUNKS,)),
        dma(()), dma((CHUNKS,)),
    ]
    hbm = pl.BlockSpec(memory_space=pltpu.HBM)
    return pl.pallas_call(
        kernel,
        out_shape=(jax.ShapeDtypeStruct((OWN, D), BF16), jax.ShapeDtypeStruct((ROWS, HD), F32)),
        in_specs=[hbm] * 6,
        out_specs=(vmem, vmem),
        scratch_shapes=scratch,
        compiler_params=pltpu.CompilerParams(
            collective_id=0, has_side_effects=True, vmem_limit_bytes=50 * 1024 * 1024
        ),
        name="attention_backward",
    )(*[pltpu.with_memory_space_constraint(one, pltpu.HBM) for one in args])


def solution(mesh):
    return jax.shard_map(
        shards,
        mesh=mesh,
        in_specs=(
            P(("dp", "tensor"), None),
            P("dp", None),
            P("dp", "tensor"),
            P("dp", "tensor"),
            P("dp", "tensor"),
            P("dp", "tensor"),
        ),
        out_specs=(P(("dp", "tensor"), None), P("dp", "tensor")),
        check_vma=False,
    )
```

time: 73.5 us -> 66.7 us (0.907); the launches traced: 72 us -> 66.6 us
  Pallas kernels: 70.1 us -> 64.6 us
    pallas_call x1, Pallas kernels: 70.1 us -> 64.6 us  [shards(): pl.pallas_call(kernel, out_shape=(jax.ShapeDtypeStruct((OWN, D), BF16), j...]
where the time goes in v3:
time: 66.7 us; the launch traced here: 66.6 us
  Pallas kernels  64.6 us (97%)
  local copies, waits for them, and re-layouts  1.33 us (2%)
    pallas_call x1, Pallas kernels, shards(): pl.pallas_call(kernel, out_shape=(jax.ShapeDtypeStruct((OWN, D), BF16), j...  64.6 us

profile of v3, /device:TPU:1, one launch (start us, length us, event | category | flops | bytes accessed | tf_op | source)
XLA Modules:
  0.0 66.6 jit_solution(5743958461578345283)
XLA Ops:
  0.6 64.6 %attention_backward.1 = (bf16[32,4608]{1,0:T(8,128)(2,1)S(1)}, f32[72,128]{1,0:T(8,128)S(1)}) custom-call(bf16[32,4608]{1,0:T(8,128)(2,1)} %normed.1, s32[1,256]{1,0:T(1,128)} %seg_hbm.1, bf16[72,256]{1,0:T(8,128)(2,1)} %w_query.1, bf16[72,128]{1,0:T(8,128)(2,1)} %w_key.1, bf16[72,128]{1,0:T(8,128)(2,1)} %w_value.1, bf16[256,256]{1,0:T(8,128)(2,1)} %grad_hbm.1), custom_call_target="tpu_custom_call" | custom-call | tf_op jit(solution)/shard_map/attention_backward/pallas_call | solution.py:482
  65.2 0.7 %copy.10 = bf16[32,4608]{1,0:T(8,128)(2,1)} copy(bf16[32,4608]{1,0:T(8,128)(2,1)S(1)} %get-tuple-element.4) | data formatting | bytes 589824
  65.9 0.6 copy.11

commit v4 on v3

--- a/solution.py
+++ b/solution.py
@@ -46,8 +46,8 @@
     seg, grad, x_buf, x_t, x_p, w_raw, w_buf, mask, q_acc, kv_acc, g_cat,
     vw, v_send, v_recv, line_sum, line_send, line_recv,
     part, sib, far_send, far_recv, near_send, near_recv,
-    in_sem, x_s, x_r, first_s, first_r, pass_s, a_r, b_r, a_end, b_end,
-    v_s, v_r, line_s, line_r, sib_s, sib_r, far_s, far_r, near_s, near_r,
+    in_sem, x_s, x_r, first_s, first_r, pass_s, a_r, b_r, end_r,
+    v_s, v_r, v_end, line_s, line_r, sib_s, sib_r, far_s, far_r, near_s, near_r,
 ):
     dp, tensor = lax.axis_index("dp"), lax.axis_index("tensor")
     y, z, x, core = dp // RING, dp % RING, tensor // 2, tensor % 2
@@ -86,7 +86,7 @@
 
     barrier = pltpu.get_barrier_semaphore()
     friends = [sibling, x_dev(1), x_dev(-1)]
-    friends += [y_dev(by) for by in range(1, RING)] + [z_dev(by) for by in range(1, RING)]
+    friends += [device(by) for device in (y_dev, z_dev) for by in (1, -1, 2, -2)]
     for friend in friends:
         pl.semaphore_signal(barrier, inc=1, device_id=friend, device_id_type=MESH)
 
@@ -123,7 +123,7 @@
         send_own(0, entry, z_dev(-ENTRIES[entry]))
         send_own(1, entry, y_dev(-ENTRIES[entry]))
     turn_own()
-    for entry in range(3, 7):
+    for entry in (3, 4):
         send_own(0, entry, z_dev(-ENTRIES[entry]))
         send_own(1, entry, y_dev(-ENTRIES[entry]))
 
@@ -157,10 +157,10 @@
 
     def relay(way):
         by = SIGN[way]
-        zz, yy = shift(z, -2 * by), shift(y, -2 * by)
-        one, two = unit_a(y, zz).at[way], unit_b(yy, z).at[way]
-        send(one, one, first_s, first_r.at[0, 7], z_dev(2 * by))
-        send(two, two, first_s, first_r.at[1, 7], y_dev(2 * by))
+        one, two = unit_a(y, shift(z, -2 * by)), unit_b(shift(y, -2 * by), z)
+        for route, unit, device in ((0, one, z_dev), (1, two, y_dev)):
+            send(unit, unit, first_s, first_r.at[route, 5 + way], device(by))
+            send(unit.at[way], unit.at[way], first_s, first_r.at[route, 7], device(2 * by))
 
     def first_arrived(entry):
         for route in range(2):
@@ -179,15 +179,15 @@
             arrived(group_bytes, a_r.at[way, hop - 1, group])
             for entry in entries:
                 unit = unit_a(yy, shift(z, ENTRIES[entry]))
-                send(unit, unit, pass_s, a_r.at[way, hop, group] if hop < 3 else a_end.at[group], y_dev(by))
+                send(unit, unit, pass_s, a_r.at[way, hop, group] if hop < 3 else end_r.at[0], y_dev(by))
             arrived(group_bytes, b_r.at[way, hop - 1, group])
             for entry in entries:
                 unit = unit_b(shift(y, ENTRIES[entry]), zz)
-                send(unit, unit, pass_s, b_r.at[way, hop, group] if hop < 3 else b_end.at[group], z_dev(by))
-
-    def pass_end(group):
-        arrived(group_bytes, a_end.at[group])
-        arrived(group_bytes, b_end.at[group])
+                send(unit, unit, pass_s, b_r.at[way, hop, group] if hop < 3 else end_r.at[1], z_dev(by))
+
+    def pass_end():
+        arrived(w_raw.at[0, 0], end_r.at[0])
+        arrived(w_raw.at[0, 0], end_r.at[1])
 
     left_half, right_half = pl.ds(0, HALF), pl.ds(HALF, HALF)
     x_right, x_left, x_far = shift(x, 1, XS), shift(x, -1, XS), shift(x, 2, XS)
@@ -204,10 +204,12 @@
         send(x_block(x_left), x_block(x_left), x_s, x_r.at[4], sibling)
         send(x_block(x_right), x_block(x_right), x_s, x_r.at[4], sibling)
 
-    def x_finish():
+    def x_share():
         for way, columns in ((2, left_half), (3, right_half)):
             arrived(x_block(x_far, columns), x_r.at[way])
             send(x_block(x_far, columns), x_block(x_far, columns), x_s, x_r.at[4], sibling)
+
+    def x_finish():
         arrived(x_buf.at[pl.ds(0, XS * OWN)], x_r.at[4])
 
     def flip(i, carry):
@@ -245,35 +247,39 @@
 
     y_pairs, z_pairs = order(y), order(z)
 
-    for entry in range(1, 7):
-        first_arrived(entry)
+    first_arrived(1)
+    first_arrived(2)
+    first_arrived(3)
+    first_arrived(4)
     pass_on(1, 0)
+    first_arrived(5)
+    first_arrived(6)
+    x_forward()
     first_arrived(7)
     pass_on(1, 1)
-    x_forward()
+    pass_on(2, 0)
     pass_on(1, 2)
-    pass_on(2, 0)
     pass_on(1, 3)
     pass_on(2, 1)
+    pass_on(3, 0)
+    x_share()
     pass_on(2, 2)
-    pass_on(3, 0)
     pass_on(2, 3)
     x_finish()
     q_acc[...] = q_product(y_pairs[0])
     pass_on(3, 1)
+    pass_on(3, 2)
     lax.fori_loop(0, CHUNKS, flip, 0)
-    pass_on(3, 2)
-    lax.fori_loop(0, CHUNKS, flip_back, 0)
     pass_on(3, 3)
     left(w_raw.at[:, 0, pl.ds(0, 7)], first_s)
     left(x_buf.at[pl.ds(0, 7 * OWN)], x_s)
+    lax.fori_loop(0, CHUNKS, flip_back, 0)
     kv_acc[...] = kv_product(z_pairs[0])
     q_acc[...] += q_product(y_pairs[1])
     kv_acc[...] += kv_product(z_pairs[1])
     q_acc[...] += q_product(y_pairs[2])
     kv_acc[...] += kv_product(z_pairs[2])
-    for group in range(RING // GROUP):
-        pass_end(group)
+    pass_end()
     kv = kv_acc[...] + kv_product(z_pairs[3])
     key, value = kv[:, :HD].astype(BF16), kv[:, HD:].astype(BF16)
     query = (q_acc[...] + q_product(y_pairs[3])).astype(BF16)
@@ -299,49 +305,50 @@
 
     routes = ((vw_y, y, y_dev), (vw_z, z, z_dev))
 
-    def vw_send(route, way, slot, device):
-        v_s_r = v_r.at[route, way, slot]
-        send(v_send.at[route, way, slot], v_recv.at[route, way, slot], v_s, v_s_r, device)
+    def vw_send(route, way, slot, sem, device, count=1):
+        one, two = [ref.at[route, way, pl.ds(slot, count)] for ref in (v_send, v_recv)]
+        send(one, two, v_s, sem, device)
 
     def vw_first():
         for way in (RIGHT, LEFT):
-            by = SIGN[way]
             for route, (own_part, position, device) in enumerate(routes):
-                v_send[route, way, 0] = own_part(shift(position, 4 * by), way).astype(BF16)
-                vw_send(route, way, 0, device(2 * by))
-                for slot, k in ((1, 1 - way), (2, way)):
+                by = SIGN[way]
+                v_send[route, way, 2] = own_part(shift(position, 4 * by), way).astype(BF16)
+                vw_send(route, way, 2, v_r.at[route, way, 1], device(2 * by))
+        for way in (RIGHT, LEFT):
+            for route, (own_part, position, device) in enumerate(routes):
+                by = SIGN[way]
+                for slot, k in ((0, 1 - way), (1, way)):
                     v_send[route, way, slot] = own_part(shift(position, 3 * by), k).astype(BF16)
-                    vw_send(route, way, slot, device(by))
-
-    def vw_near():
-        for way in (RIGHT, LEFT):
-            by = SIGN[way]
+                    vw_send(route, way, slot, v_r.at[route, way, slot], device(by))
+        for way in (RIGHT, LEFT):
             for route, (own_part, position, device) in enumerate(routes):
+                by = SIGN[way]
                 for k in range(2):
                     v_send[route, way, 5 + k] = own_part(shift(position, by), k).astype(BF16)
-                    vw_send(route, way, 5 + k, device(by))
-
-    def vw_second():
-        for way in (RIGHT, LEFT):
-            by = SIGN[way]
+                vw_send(route, way, 5, v_end.at[route], device(by), 2)
+
+    def vw_second(long):
+        for way in (RIGHT, LEFT):
             for route, (own_part, position, device) in enumerate(routes):
-                for slot, k, gets in ((3, 1 - way, (1,)), (4, way, (0, 2))):
-                    total = own_part(shift(position, 2 * by), k)
-                    for got in gets:
-                        arrived(v_send.at[0, 0, 0], v_r.at[route, way, got])
-                        total = total + v_recv[route, way, got].astype(F32)
-                    v_send[route, way, slot] = total.astype(BF16)
-                    vw_send(route, way, slot, device(2 * by))
+                by, k = SIGN[way], way if long else 1 - way
+                total = own_part(shift(position, 2 * by), k)
+                gets = (1, 2) if long else (0,)
+                arrived(v_send.at[0, 0, pl.ds(0, len(gets))], v_r.at[route, way, int(long)])
+                for got in gets:
+                    total = total + v_recv[route, way, got].astype(F32)
+                v_send[route, way, 3 + k] = total.astype(BF16)
+                vw_send(route, way, 3 + k, v_end.at[route], device(2 * by))
 
     y_first = z // 4 == y % 2
 
     def vw_turn():
         for route, (own_part, position, _) in enumerate(routes):
+            arrived(v_send.at[0, :, pl.ds(3, 4)], v_end.at[route])
             for k in range(2):
                 total = own_part(position, k)
                 for way in (RIGHT, LEFT):
-                    for slot in (5 + k, 4 if k == way else 3):
-                        arrived(v_send.at[0, 0, 0], v_r.at[route, way, slot])
+                    for slot in (5 + k, 3 + k):
                         total = total + v_recv[route, way, slot].astype(F32)
                 total = total.reshape(2, ROWS, HD)
                 at_rows = pl.ds(4 * route + 2 * k, 2)
@@ -364,7 +371,6 @@
         value_grad[...] = total * float(TOK * RING * RING) ** (-0.5)
 
     vw_first()
-    vw_near()
 
     dscores = []
     for h in range(2):
@@ -379,7 +385,8 @@
     def ig_part(q):
         both = dot_nt(g_cat[...], weights((0, 1, 2, 3), q)).astype(BF16)
         part[q] = both.reshape(XS, 2, OWN, CHUNK)
-        send(part.at[q, :, other], sib.at[q], sib_s, sib_r.at[q], sibling)
+        for xx, sem in ((x_far, 0), (x_right, 1), (x_left, 1), (x, 1)):
+            send(part.at[q, xx, other], sib.at[q, xx], sib_s, sib_r.at[sem, q], sibling)
 
     def chip_sum(q, xx):
         return part[q, xx, core].astype(F32) + sib[q, xx].astype(F32)
@@ -388,12 +395,13 @@
         send(near_send.at[q, way], near_recv.at[q, way], near_s, near_r.at[q], x_dev(SIGN[way]))
 
     def ig_far(q):
-        arrived(sib.at[q], sib_r.at[q])
+        arrived(sib.at[q, 0], sib_r.at[0, q])
         far_send[q] = chip_sum(q, x_far).astype(BF16)
         send(far_send.at[q], far_recv.at[q], far_s, far_r.at[q], x_dev(SIGN[q % 2]))
 
     def ig_near(q):
         way = 1 - q % 2
+        arrived(sib.at[q, pl.ds(0, 3)], sib_r.at[1, q])
         near_send[q, way] = chip_sum(q, shift(x, SIGN[way], XS)).astype(BF16)
         near(q, way)
 
@@ -415,28 +423,29 @@
     ig_part(2)
     ig_far(0)
     ig_part(3)
+    vw_second(False)
     ig_far(1)
     ig_far(2)
     ig_near(0)
     ig_near(1)
     ig_far(3)
+    vw_second(True)
     ig_near(2)
     ig_near(3)
-    vw_second()
     ig_second(0)
     ig_second(1)
     ig_second(2)
+    vw_turn()
     ig_second(3)
-    vw_turn()
     left(w_raw.at[:, :, pl.ds(0, 7)], pass_s)
     left(v_send, v_s)
     left(sib, sib_s)
     left(far_send, far_s)
     ig_finish(0)
     ig_finish(1)
+    ig_finish(2)
     vw_finish()
     left(line_recv.at[pl.ds(0, RING - 1)], line_s)
-    ig_finish(2)
     ig_finish(3)
     left(near_send, near_s)
 
@@ -471,10 +480,10 @@
         dma((5,)),
         dma(()), dma((5,)),
         dma(()), dma((2, RING)),
-        dma(()), dma((2, 3, 4)), dma((2, 3, 4)), dma((4,)), dma((4,)),
-        dma(()), dma((2, 2, 7)),
+        dma(()), dma((2, 3, 4)), dma((2, 3, 4)), dma((2,)),
+        dma(()), dma((2, 2, 2)), dma((2,)),
         dma(()), dma(()),
-        dma(()), dma((CHUNKS,)),
+        dma(()), dma((2, CHUNKS)),
         dma(()), dma((CHUNKS,)),
         dma(()), dma((CHUNKS,)),
     ]

time: 66.7 us -> 63.8 us (0.957)
  the two profiles are of different devices: /device:TPU:1 before, /device:TPU:2 now
where the time goes in v4:
time: 63.8 us; the launch traced here: 63.7 us
  Pallas kernels  61.7 us (97%)
  local copies, waits for them, and re-layouts  1.33 us (2%)
  between operations  0.64 us (1%)
    pallas_call x1, Pallas kernels, shards(): pl.pallas_call(kernel, out_shape=(jax.ShapeDtypeStruct((OWN, D), BF16), j...  61.7 us
    unnamed x2, local copies, waits for them, and re-layouts  1.33 us

profile of v4, /device:TPU:2, one launch (start us, length us, event | category | flops | bytes accessed | tf_op | source)
XLA Modules:
  0.0 63.7 jit_solution(8125829255701624906)
XLA Ops:
  0.6 61.7 %attention_backward.1 = (bf16[32,4608]{1,0:T(8,128)(2,1)S(1)}, f32[72,128]{1,0:T(8,128)S(1)}) custom-call(bf16[32,4608]{1,0:T(8,128)(2,1)} %normed.1, s32[1,256]{1,0:T(1,128)} %seg_hbm.1, bf16[72,256]{1,0:T(8,128)(2,1)} %w_query.1, bf16[72,128]{1,0:T(8,128)(2,1)} %w_key.1, bf16[72,128]{1,0:T(8,128)(2,1)} %w_value.1, bf16[256,256]{1,0:T(8,128)(2,1)} %grad_hbm.1), custom_call_target="tpu_custom_call" | custom-call | tf_op jit(solution)/shard_map/attention_backward/pallas_call | solution.py:491
  62.4 0.7 %copy.10 = bf16[32,4608]{1,0:T(8,128)(2,1)} copy(bf16[32,4608]{1,0:T(8,128)(2,1)S(1)} %get-tuple-element.4) | data formatting | bytes 589824
  63.1 0.6 copy.11

commit v5 on v4

--- a/solution.py
+++ b/solution.py
@@ -448,6 +448,17 @@
     left(line_recv.at[pl.ds(0, RING - 1)], line_s)
     ig_finish(3)
     left(near_send, near_s)
+
+
+def store(input_grad, value_grad, input_grad_out, value_grad_out, sems):
+    copies = [
+        pltpu.make_async_copy(input_grad, input_grad_out, sems.at[0]),
+        pltpu.make_async_copy(value_grad, value_grad_out, sems.at[1]),
+    ]
+    for one in copies:
+        one.start()
+    for one in copies:
+        one.wait()
 
 
 def shards(*args):
@@ -488,7 +499,7 @@
         dma(()), dma((CHUNKS,)),
     ]
     hbm = pl.BlockSpec(memory_space=pltpu.HBM)
-    return pl.pallas_call(
+    results = pl.pallas_call(
         kernel,
         out_shape=(jax.ShapeDtypeStruct((OWN, D), BF16), jax.ShapeDtypeStruct((ROWS, HD), F32)),
         in_specs=[hbm] * 6,
@@ -499,6 +510,15 @@
         ),
         name="attention_backward",
     )(*[pltpu.with_memory_space_constraint(one, pltpu.HBM) for one in args])
+    return pl.pallas_call(
+        store,
+        out_shape=(jax.ShapeDtypeStruct((OWN, D), BF16), jax.ShapeDtypeStruct((ROWS, HD), F32)),
+        in_specs=[vmem] * 2,
+        out_specs=(hbm, hbm),
+        scratch_shapes=[dma((2,))],
+        compiler_params=pltpu.CompilerParams(vmem_limit_bytes=4 * 1024 * 1024),
+        name="store",
+    )(*results)
 
 
 def solution(mesh):

time: 63.8 us -> 63.2 us (level)
  local copies, waits for them, and re-layouts: 1.33 us -> 0 us
  Pallas kernels: 61.7 us -> 62.5 us
    unnamed x2 -> x0, local copies, waits for them, and re-layouts: 1.33 us -> none
    pallas_call x0 -> x1, Pallas kernels: none -> 0.74 us  [shards(): pl.pallas_call(store, out_shape=(jax.ShapeDtypeStruct((OWN, D), BF16), ja...]
where the time goes in v5:
time: 63.2 us; the launch traced here: 63.1 us
  Pallas kernels  62.5 us (99%)
  between operations  0.64 us (1%)
    pallas_call x1, Pallas kernels, shards(): pl.pallas_call(kernel, out_shape=(jax.ShapeDtypeStruct((OWN, D), BF16), j...  61.7 us

profile of v5, /device:TPU:2, one launch (start us, length us, event | category | flops | bytes accessed | tf_op | source)
XLA Modules:
  0.0 63.1 jit_solution(7090131846388704889)
XLA Ops:
  0.6 61.7 %attention_backward.1 = (bf16[32,4608]{1,0:T(8,128)(2,1)S(1)}, f32[72,128]{1,0:T(8,128)S(1)}) custom-call(bf16[32,4608]{1,0:T(8,128)(2,1)} %normed.1, s32[1,256]{1,0:T(1,128)} %seg_hbm.1, bf16[72,256]{1,0:T(8,128)(2,1)} %w_query.1, bf16[72,128]{1,0:T(8,128)(2,1)} %w_key.1, bf16[72,128]{1,0:T(8,128)(2,1)} %w_value.1, bf16[256,256]{1,0:T(8,128)(2,1)} %grad_hbm.1), custom_call_target="tpu_custom_call" | custom-call | tf_op jit(solution)/shard_map/attention_backward/pallas_call | solution.py:502
  62.4 0.7 %store.1 = (bf16[32,4608]{1,0:T(8,128)(2,1)}, f32[72,128]{1,0:T(8,128)}) custom-call(bf16[32,4608]{1,0:T(8,128)(2,1)S(1)} %get-tuple-element.4.input_grad, f32[72,128]{1,0:T(8,128)S(1)} %get-tuple-element.5.value_grad), custom_call_target="tpu_custom_call" | custom-call | tf_op jit(solution)/shard_map/store/pallas_call | solution.py:513

commit v6 on v5

--- a/solution.py
+++ b/solution.py
@@ -108,30 +108,47 @@
 
     pl.semaphore_wait(barrier, len(friends))
 
-    def send_own(route, entry, device):
-        for i in range(2):
-            send(own[2 * route + i], w_raw.at[route, y, z, i], first_s, first_r.at[route, entry], device)
-
-    def turn_own():
-        for i in range(2):
-            for way in (RIGHT, LEFT):
-                by = SIGN[way]
-                send(own[i], own_a.at[i], pass_s, a_r.at[way, 0, 0], y_dev(by))
-                send(own[2 + i], own_b.at[i], pass_s, b_r.at[way, 0, 0], z_dev(by))
-
-    for entry in (1, 2):
-        send_own(0, entry, z_dev(-ENTRIES[entry]))
-        send_own(1, entry, y_dev(-ENTRIES[entry]))
-    turn_own()
-    for entry in (3, 4):
-        send_own(0, entry, z_dev(-ENTRIES[entry]))
-        send_own(1, entry, y_dev(-ENTRIES[entry]))
-
+    def unit_a(yy, zz):
+        return w_raw.at[0, yy, zz]
+
+    def unit_b(yy, zz):
+        return w_raw.at[1, yy, zz]
+
+    def turn(entry):
+        zz, yy = shift(z, ENTRIES[entry]), shift(y, ENTRIES[entry])
+        for way in (RIGHT, LEFT):
+            by, slot = SIGN[way], (way, 0, entry // GROUP)
+            send(unit_a(y, zz), unit_a(y, zz), pass_s, a_r.at[slot], y_dev(by))
+            send(unit_b(yy, z), unit_b(yy, z), pass_s, b_r.at[slot], z_dev(by))
+
+    def relay(way):
+        by = SIGN[way]
+        one, two = unit_a(y, shift(z, -2 * by)), unit_b(shift(y, -2 * by), z)
+        for route, unit, device in ((0, one, z_dev), (1, two, y_dev)):
+            send(unit, unit, first_s, first_r.at[route, 5 + way], device(by))
+            send(unit.at[way], unit.at[way], first_s, first_r.at[route, 7], device(2 * by))
+
+    def first_arrived(entry):
+        for route in range(2):
+            arrived(own_a, first_r.at[route, entry])
+        if entry in (3, 4):
+            relay(entry - 3)
+        turn(entry)
+
+    def send_own(entry):
+        send(own_a, own_a, first_s, first_r.at[0, entry], z_dev(-ENTRIES[entry]))
+        send(own_b, own_b, first_s, first_r.at[1, entry], y_dev(-ENTRIES[entry]))
+
+    pltpu.make_async_copy(own_a, own_a, in_sem.at[0]).wait()
+    pltpu.make_async_copy(own_b, own_b, in_sem.at[1]).wait()
+    send_own(1)
+    send_own(2)
+    turn(0)
+    send_own(3)
+    send_own(4)
     send(normed, here, x_s, x_r.at[0], x_dev(1))
     send(normed, here, x_s, x_r.at[1], x_dev(-1))
     send(normed, here, x_s, x_r.at[4], sibling)
-    pltpu.make_async_copy(own_a, own_a, in_sem.at[0]).wait()
-    pltpu.make_async_copy(own_b, own_b, in_sem.at[1]).wait()
     for one in local[4:]:
         one.wait()
 
@@ -141,33 +158,6 @@
     key_at = lax.broadcasted_iota(jnp.int32, (TOK, TOK), 0)
     query_at = lax.broadcasted_iota(jnp.int32, (TOK, TOK), 1)
     mask[...] = jnp.where((key_at <= query_at) & (seg_col == seg_f), 1.0, 0.0).astype(F32)
-
-    def unit_a(yy, zz):
-        return w_raw.at[0, yy, zz]
-
-    def unit_b(yy, zz):
-        return w_raw.at[1, yy, zz]
-
-    def turn(entry):
-        zz, yy = shift(z, ENTRIES[entry]), shift(y, ENTRIES[entry])
-        for way in (RIGHT, LEFT):
-            by, slot = SIGN[way], (way, 0, entry // GROUP)
-            send(unit_a(y, zz), unit_a(y, zz), pass_s, a_r.at[slot], y_dev(by))
-            send(unit_b(yy, z), unit_b(yy, z), pass_s, b_r.at[slot], z_dev(by))
-
-    def relay(way):
-        by = SIGN[way]
-        one, two = unit_a(y, shift(z, -2 * by)), unit_b(shift(y, -2 * by), z)
-        for route, unit, device in ((0, one, z_dev), (1, two, y_dev)):
-            send(unit, unit, first_s, first_r.at[route, 5 + way], device(by))
-            send(unit.at[way], unit.at[way], first_s, first_r.at[route, 7], device(2 * by))
-
-    def first_arrived(entry):
-        for route in range(2):
-            arrived(own_a, first_r.at[route, entry])
-        if entry in (3, 4):
-            relay(entry - 3)
-        turn(entry)
 
     group_bytes = w_raw.at[0, 0, pl.ds(0, GROUP)]
 
@@ -295,13 +285,13 @@
     grad_v = (dot(rounded[0], grad[:, :HD]) + dot(rounded[1], grad[:, HD:])).astype(BF16)
 
     for yy in range(RING):
-        vw[yy // 2, yy % 2] = dot(x_t[yy].reshape(UNIT, TOK), grad_v).reshape(RING, ROWS, HD)
+        vw[yy // 2, yy % 2] = dot(x_t[yy].reshape(UNIT, TOK), grad_v).reshape(RING // 2, 2, ROWS, HD)
 
     def vw_y(yy, k):
-        return vw[yy // 2, yy % 2, pl.ds(4 * (yy % 2) + 2 * k, 2)].reshape(PAIR, HD)
+        return vw[yy // 2, yy % 2, 2 * k : 2 * k + 2, yy % 2].reshape(PAIR, HD)
 
     def vw_z(zz, k):
-        return vw[2 * k : 2 * k + 2, 1 - zz // 4, zz].reshape(PAIR, HD)
+        return vw[2 * k : 2 * k + 2, 1 - zz % 2, zz // 2, zz % 2].reshape(PAIR, HD)
 
     routes = ((vw_y, y, y_dev), (vw_z, z, z_dev))
 
@@ -340,7 +330,7 @@
                 v_send[route, way, 3 + k] = total.astype(BF16)
                 vw_send(route, way, 3 + k, v_end.at[route], device(2 * by))
 
-    y_first = z // 4 == y % 2
+    y_first = z % 2 == y % 2
 
     def vw_turn():
         for route, (own_part, position, _) in enumerate(routes):
@@ -356,7 +346,7 @@
                 padded = jnp.concatenate([total, jnp.zeros((2, PADDED - ROWS, HD), F32)], axis=1)
                 line_send[at_rows] = padded.astype(BF16)
         for i in range(4):
-            zz, yy = 4 * (y % 2) + i, 2 * i + 1 - z // 4
+            zz, yy = 2 * i + y % 2, 2 * i + 1 - z % 2
             one = copy(line_send.at[i], line_recv.at[z], line_s, line_r, at(x, y, zz, core))
             two = copy(line_send.at[4 + i], line_recv.at[y], line_s, line_r, at(x, yy, z, core))
             pl.when(zz != z)(one.start)
@@ -365,7 +355,7 @@
     def vw_finish():
         arrived(line_recv.at[pl.ds(0, RING - 1)], line_r)
         position = jnp.where(y_first, z, y)
-        total = line_sum[jnp.where(y_first, z % 4, 4 + y // 2)]
+        total = line_sum[jnp.where(y_first, z // 2, 4 + y // 2)]
         for by in range(1, RING):
             total = total + line_recv[shift(position, by)].astype(F32)[:ROWS]
         value_grad[...] = total * float(TOK * RING * RING) ** (-0.5)
@@ -423,12 +413,12 @@
     ig_part(2)
     ig_far(0)
     ig_part(3)
+    ig_far(1)
     vw_second(False)
-    ig_far(1)
     ig_far(2)
+    ig_far(3)
     ig_near(0)
     ig_near(1)
-    ig_far(3)
     vw_second(True)
     ig_near(2)
     ig_near(3)
@@ -476,7 +466,7 @@
         pltpu.VMEM((TOK, 2 * HD), F32),
         pltpu.VMEM((TOK, 2 * HD), F32),
         pltpu.VMEM((TOK, 4 * HD), BF16),
-        pltpu.VMEM((RING // 2, 2, RING, ROWS, HD), F32),
+        pltpu.VMEM((RING // 2, 2, RING // 2, 2, ROWS, HD), F32),
         pltpu.VMEM((2, 2, 7, PAIR, HD), BF16),
         pltpu.VMEM((2, 2, 7, PAIR, HD), BF16),
         pltpu.VMEM((RING, ROWS, HD), F32),

time: 63.2 us -> 63 us (level)
  the two profiles are of different devices: /device:TPU:2 before, /device:TPU:8 now
where the time goes in v6:
time: 63 us; the launch traced here: 62.9 us
  Pallas kernels  62.2 us (99%)
  between operations  0.64 us (1%)
    pallas_call x1, Pallas kernels, shards(): pl.pallas_call(kernel, out_shape=(jax.ShapeDtypeStruct((OWN, D), BF16), j...  61.5 us

profile of v6, /device:TPU:8, one launch (start us, length us, event | category | flops | bytes accessed | tf_op | source)
XLA Modules:
  0.0 62.9 jit_solution(8550948203757753503)
XLA Ops:
  0.6 61.5 %attention_backward.1 = (bf16[32,4608]{1,0:T(8,128)(2,1)S(1)}, f32[72,128]{1,0:T(8,128)S(1)}) custom-call(bf16[32,4608]{1,0:T(8,128)(2,1)} %normed.1, s32[1,256]{1,0:T(1,128)} %seg_hbm.1, bf16[72,256]{1,0:T(8,128)(2,1)} %w_query.1, bf16[72,128]{1,0:T(8,128)(2,1)} %w_key.1, bf16[72,128]{1,0:T(8,128)(2,1)} %w_value.1, bf16[256,256]{1,0:T(8,128)(2,1)} %grad_hbm.1), custom_call_target="tpu_custom_call" | custom-call | tf_op jit(solution)/shard_map/attention_backward/pallas_call | solution.py:492
  62.1 0.7 %store.1 = (bf16[32,4608]{1,0:T(8,128)(2,1)}, f32[72,128]{1,0:T(8,128)}) custom-call(bf16[32,4608]{1,0:T(8,128)(2,1)S(1)} %get-tuple-element.4.input_grad, f32[72,128]{1,0:T(8,128)S(1)} %get-tuple-element.5.value_grad), custom_call_target="tpu_custom_call" | custom-call | tf_op jit(solution)/shard_map/store/pallas_call | solution.py:503
